TPU v7x, 512 devices: a whole 4x8x8 slice. The times are simulated.
512 devices in a mesh: path: 16 (over z, core), trade: 32 (over x, y).
Axes of the slice: x: 4, y: 8, z: 8, core: 2. Of those that a mesh axis runs over, the one named last changes fastest.
Arguments:
- basis: bfloat16 [2, 2048, 64], P(None, 'path'), may hold values from -6 to 6
- fx_rates: float32 [2, 2048, 16], P(None, 'path'), may hold values from 0.5 to 2
- coefficients: bfloat16 [64, 131072], P(None, 'trade'), may hold values from -0.375 to 0.375
- unwind_worth_minimum: float32 [131072], P('trade'), may hold values from -0.3 to 0
- position_offset_group: int32 [131072], P('trade'), may hold values from 0 to 2047
- currency: int32 [131072], P('trade'), may hold values from 0 to 15
Outputs:
- exposure: float32 [2, 2048, 2048], P(None, 'path', 'trade')
- expected_exposure: float32 [2, 2048], P(None, 'trade')
All inputs are finite; a program needn't handle non-finite values.
Results may differ from a plain program's by a relative error of at most 0.0006.
Values sent between devices are 32-bit elements; how exact they have to be, the bound alone decides.
No kernel may reach another device: no remote copies, remote signals or barrier semaphores. Data moves between devices by JAX's collectives and lax.ppermute only.
A program may use at most 64 MiB of HBM per device.

v0:
```python
import jax
import jax.numpy as jnp
from jax import lax
from jax.sharding import PartitionSpec as P

NF = 16
SET_DEV = 64


def shards(basis, fx_rates, coefficients, unwind_worth_minimum, position_offset_group, currency):
    highest = lax.Precision.HIGHEST
    dates = basis.shape[0]
    local_path_rows = basis.shape[1]
    total_paths = local_path_rows * lax.axis_size("path")
    total_sets = SET_DEV * lax.axis_size("trade")
    basis_wide = basis.astype(jnp.float32)
    normal_matrix_partial = jnp.einsum(
        "dpk,dpl->dkl", basis, basis, preferred_element_type=jnp.float32
    )
    gram = lax.psum(normal_matrix_partial, "path")
    cur_table = (currency[:, None] == jnp.arange(NF, dtype=jnp.int32)[None, :]).astype(jnp.float32)
    worth_computed = []
    for date in range(dates):
        fitted_regressor_guess = jnp.dot(
            basis[date], coefficients, preferred_element_type=jnp.float32
        )
        market_rate = jnp.dot(fx_rates[date], cur_table.T, precision=highest)
        worth_computed.append(
            (
                market_rate * jnp.maximum(fitted_regressor_guess, unwind_worth_minimum[None, :])
            ).astype(jnp.bfloat16)
        )
    position_worths = jnp.stack(worth_computed)
    set_ids = jnp.arange(total_sets, dtype=jnp.int32)
    set_table = (position_offset_group[:, None] == set_ids[None, :]).astype(jnp.bfloat16)
    netted = lax.psum_scatter(
        jnp.einsum("dpt,ts->sdp", position_worths, set_table, preferred_element_type=jnp.float32),
        "trade",
        scatter_dimension=0,
        tiled=True,
    )
    moment_local = jnp.einsum("dpk,sdp->sdk", basis_wide, netted, precision=highest)
    moments = lax.psum(moment_local, "path")
    solved_coefficient = []
    for date in range(dates):
        factor = jnp.linalg.cholesky(gram[date])
        solved_coefficient.append(jax.scipy.linalg.cho_solve((factor, True), moments[:, date, :].T))
    beta = jnp.stack(solved_coefficient)
    smooth = jnp.einsum("dpk,dks->dps", basis_wide, beta, precision=highest)
    exposure = jnp.maximum(smooth, 0.0)
    summed = lax.psum(jnp.sum(exposure, axis=1), "path")
    return (exposure, summed / total_paths)


def solution(mesh):
    return jax.shard_map(
        shards,
        mesh=mesh,
        in_specs=(
            P(None, "path", None),
            P(None, "path", None),
            P(None, "trade"),
            P("trade"),
            P("trade"),
            P("trade"),
        ),
        out_specs=(P(None, "path", "trade"), P(None, "trade")),
        check_vma=False,
    )
```

profile of v0, /device:TPU:4, one launch (start us, length us, event | category | flops | bytes accessed | tf_op | source)
XLA Modules:
  0.0 429.3 jit_solution(10726540263731322645)
XLA Ops:
  7.2 0.0 copy-start
  7.2 0.0 copy-start.4
  7.2 0.0 copy-start.2
  7.2 0.0 copy-start.3
  7.2 0.0 copy-start.1
  7.2 0.0 reduce-scatter.2.cloned.1.call-start
  7.3 2.6 convolution_bitcast_fusion
  9.9 0.0 copy-done.4
  9.9 0.0 copy-done.2
  9.9 1.8 convolution_bitcast_fusion.1
  11.7 0.0 copy-done
  11.7 0.0 copy-done.3
  11.7 0.0 copy-done.1
  11.8 1.2 fusion.8
  13.0 0.0 copy-start.5
  13.0 1.0 fusion.9
  14.1 0.0 copy-done.5
  14.1 10.9 %fusion.1 = f32[2048,2,128]{2,0,1:T(8,128)} fusion(s32[4096]{0:T(1024)S(1)} %copy-done.5, bf16[1,128,4096]{1,2,0:T(8,128)(2,1)S(1)} %fusion.8, bf16[1,128,4096]{1,2,0:T(8,128)(2,1)S(1)} %fusion.9), kind=kOutput, calls=%fused_computation.2 | convolution fusion | flops 4307550208 | bytes 4210688 | tf_op jit(solution)/shard_map/dpt,ts->sdp/dot_general | solution.py:37
  24.9 0.0 reduce-scatter.2.cloned.1.call-update
  25.0 0.3 all-reduce.3.cloned.1.call-start
  25.2 0.8 fusion.40
  26.0 223.8 %reduce-scatter.2.cloned.1.call-done = f32[64,2,128]{2,0,1:T(8,128)} async-done(((f32[2048,2,128]{2,0,1:T(8,128)}), f32[64,2,128]{2,0,1:T(8,128)}) %reduce-scatter.2.cloned.1.call-update) | async-done | bytes 65552 | tf_op jit(solution)/shard_map/reduce_scatter | solution.py:36
  249.8 1.6 convolution_bitcast_fusion.2
  251.4 0.0 all-reduce.3.cloned.1.call-update
  251.4 115.0 %all-reduce.3.cloned.1.call-done = (f32[64,2,64]{2,0,1:T(8,128)}, f32[2,64,64]{1,2,0:T(8,128)}) async-done(((f32[64,2,64]{2,0,1:T(8,128)}, f32[2,64,64]{1,2,0:T(8,128)}), (f32[64,2,64]{2,0,1:T(8,128)}, f32[2,64,64]{1,2,0:T(8,128)})) %all-reduce.3.cloned.1.call-update) | async-done | bytes 65552 | tf_op jit(solution)/shard_map/psum | solution.py:43
  366.4 0.8 slice_bitcast_fusion.5
  367.2 0.1 copy.15
  367.3 0.1 copy.18
  367.3 0.8 fusion.24
  368.1 5.8 %cholesky.44 = f32[64,64]{1,0:T(8,128)S(1)} custom-call(f32[64,64]{1,0:T(8,128)S(1)} %get-tuple-element.6), custom_call_target="Cholesky" | custom-call | tf_op jit(solution)/shard_map/jit(cholesky)/cholesky | solution.py:46
  374.0 0.6 compare_reduce_fusion.1
  374.7 0.7 fusion.19
  375.3 4.9 %custom-call.8 = f32[1,64,64]{1,2,0:T(8,128)S(1)} custom-call(f32[1,64,64]{2,1,0:T(8,128)S(1)} %fusion.19), custom_call_target="InvertDiagBlocksLowerTriangular" | custom-call | tf_op jit(solution)/shard_map/jit(_cho_solve)/triangular_solve | solution.py:47
  380.2 1.0 fusion.22
  381.2 0.2 convolution_bitcast_fusion.4
  381.4 5.8 %cholesky.55 = f32[64,64]{1,0:T(8,128)S(1)} custom-call(f32[64,64]{1,0:T(8,128)S(1)} %get-tuple-element.7), custom_call_target="Cholesky" | custom-call | tf_op jit(solution)/shard_map/jit(cholesky)/cholesky | solution.py:46
  387.3 0.6 compare_reduce_fusion
  387.9 0.7 fusion.20
  388.6 4.9 %custom-call.9 = f32[1,64,64]{1,2,0:T(8,128)S(1)} custom-call(f32[1,64,64]{2,1,0:T(8,128)S(1)} %fusion.20), custom_call_target="InvertDiagBlocksLowerTriangular" | custom-call | tf_op jit(solution)/shard_map/jit(_cho_solve)/triangular_solve | solution.py:47
  393.5 1.0 fusion.21
  394.5 0.2 convolution_bitcast_fusion.3
  394.7 0.9 fusion.39
  395.5 26.4 %psum.23 = f32[2,64]{1,0:T(2,128)S(1)} all-reduce(f32[2,64]{1,0:T(2,128)S(1)} %get-tuple-element.10), channel_id=1, replica_groups=mesh['path'=16,'trade'=32] {'path'}, use_global_device_ids=true, to_apply=%region_6.9 | all-reduce | flops 128 | bytes 1024 | tf_op jit(solution)/shard_map/psum | solution.py:51
  421.9 0.6 broadcast_multiply_fusion
  (2 shorter events, 0.1 us)
Async XLA Ops:
  7.2 4.6 %copy-start = (bf16[64,4096]{1,0:T(8,128)(2,1)S(1)}, bf16[64,4096]{1,0:T(8,128)(2,1)}, u32[]{:S(2)}) copy-start(bf16[64,4096]{1,0:T(8,128)(2,1)} %param.11) | copy-start | bytes 1572868
  7.2 2.7 copy-start.4
  7.2 2.7 copy-start.2
  7.2 4.5 %copy-start.3 = (f32[4096]{0:T(1024)S(1)}, f32[4096]{0:T(1024)}, u32[]{:S(2)}) copy-start(f32[4096]{0:T(1024)} %param.12) | copy-start | bytes 49156
  7.2 4.5 %copy-start.1 = (bf16[2,128,64]{1,2,0:T(8,128)(2,1)S(1)}, bf16[2,128,64]{1,2,0:T(8,128)(2,1)}, u32[]{:S(2)}) copy-start(bf16[2,128,64]{1,2,0:T(8,128)(2,1)} %param.9) | copy-start | bytes 98308
  7.2 242.5 %reduce-scatter.2.cloned.1.call-start = ((), (), s32[]{:S(2)}) async-start(), calls=%async_computation.1 | async-start | bytes 2162688 | tf_op jit(solution)/shard_map/reduce_scatter | solution.py:36
  13.0 1.1 copy-start.5
  25.0 341.4 %all-reduce.3.cloned.1.call-start = ((), (), s32[]{:S(2)}) async-start(), calls=%async_computation.2 | async-start | bytes 262144 | tf_op jit(solution)/shard_map/psum | solution.py:43
Sparse Core Ops, SparseCore 0:
  25.1 224.6 reduce-scatter.1
  252.8 113.5 all-reduce.2
where the time goes:
time: 430 us; the launch traced here: 429 us
  waiting for transfers between devices  339 us (79%)
  blocking collectives  26.4 us (6%)
  other arithmetic  25.5 us (6%)
  matrix products  23.2 us (5%)
  between operations  14.2 us (3%)
    reduce_scatter x1, waiting for transfers between devices, shards(): lax.psum_scatter(jnp.einsum('dpt,ts->sdp', position_worths, set_table, pr...  224 us
    psum x1, waiting for transfers between devices, shards(): moments = lax.psum(moment_local, 'path')  115 us
    psum x1, blocking collectives, shards(): summed = lax.psum(jnp.sum(exposure, axis=1), 'path')  26.4 us
    another operation x6, other arithmetic, shards(): factor = jnp.linalg.cholesky(gram[date])  13 us
    another operation x4, other arithmetic, shards(): jax.scipy.linalg.cho_solve((factor, True), moments[:, date, :].T)  11.1 us
    dot_general x1, matrix products, shards(): jnp.einsum('dpt,ts->sdp', position_worths, set_table, preferred_element_t...  10.9 us
  transfers between devices with their start and end apart: 2, of which 2 were waited for; matrix products, arithmetic and copies ran while one was open for 0% of the time, Pallas kernels for 0%

commit v1 on v0

v1 whole, which is shorter than its diff:
```python
import jax
import jax.numpy as jnp
from jax import lax
from jax.experimental import pallas as pl
from jax.experimental.pallas import tpu as pltpu
from jax.sharding import Mesh, PartitionSpec as P

F32 = jnp.float32
BF16 = jnp.bfloat16
HIGHEST = lax.Precision.HIGHEST
DATES = 2
K = 64
NF = 16
SETS = 2048
PATHS = 2048
OWNERS = 32
SET_DEV = SETS // OWNERS
HALF = SET_DEV // 2
LANES = DATES * K
TILE = 1024
VMEM = pl.BlockSpec(memory_space=pltpu.VMEM)
SMEM = pl.BlockSpec(memory_space=pltpu.SMEM)


def split(x):
    high = x.astype(BF16)
    rest = x - high.astype(F32)
    middle = rest.astype(BF16)
    low = (rest - middle.astype(F32)).astype(BF16)
    return high, middle, low


def dot_nt(a, b, precision=None):
    return lax.dot_general(
        a, b, (((1,), (1,)), ((), ())), precision=precision, preferred_element_type=F32
    )


def dot_tn(a, b, precision=None):
    return lax.dot_general(
        a, b, (((0,), (0,)), ((), ())), precision=precision, preferred_element_type=F32
    )


def block_diagonal(a, b):
    return jnp.concatenate(
        [
            jnp.concatenate([a, jnp.zeros((a.shape[0], b.shape[1]), a.dtype)], axis=1),
            jnp.concatenate([jnp.zeros((b.shape[0], a.shape[1]), b.dtype), b], axis=1),
        ],
        axis=0,
    )


def half_moments(half, basis_ref, value_ref, group_ref, out_ref, total_ref):
    rows = OWNERS * HALF
    trades = value_ref.shape[1]
    for i in range(trades // TILE):
        span = pl.ds(i * TILE, TILE)
        group = group_ref[:, span]
        row = jnp.where(
            (group // HALF) % 2 == half, (group // SET_DEV) * HALF + group % HALF, -1
        )
        member = lax.broadcasted_iota(jnp.int32, (rows, TILE), 0) == row
        part = dot_nt(jnp.where(member, 1.0, 0.0).astype(BF16), value_ref[:, span])
        if i == 0:
            total_ref[...] = part
        else:
            total_ref[...] += part
    wide = block_diagonal(basis_ref[0], basis_ref[1])
    step = 256
    for i in range(rows // step):
        span = pl.ds(i * step, step)
        high, middle, low = split(total_ref[span, :])
        moments = (
            jnp.dot(high, wide, preferred_element_type=F32)
            + jnp.dot(middle, wide, preferred_element_type=F32)
            + jnp.dot(low, wide, preferred_element_type=F32)
        )
        out_ref[pl.ds(i * step // HALF, step // HALF)] = moments.reshape(
            step // HALF, HALF, LANES
        )


def send_kernel(
    core_ref, basis_ref, fx_ref, coef_ref, floor_ref, group_ref, currency_ref,
    out_ref, value_ref, total_ref,
):
    paths = basis_ref.shape[1]
    trades = coef_ref.shape[1]
    basis = basis_ref[...].reshape(DATES * paths, K)
    rates = jnp.concatenate(split(fx_ref[...].reshape(DATES * paths, NF)), axis=1)
    for i in range(trades // TILE):
        span = pl.ds(i * TILE, TILE)
        fitted = jnp.dot(basis, coef_ref[:, span], preferred_element_type=F32)
        names = lax.broadcasted_iota(jnp.int32, (3 * NF, TILE), 0) % NF
        chosen = jnp.where(names == currency_ref[:, span], 1.0, 0.0).astype(BF16)
        rate = jnp.dot(rates, chosen, preferred_element_type=F32)
        value_ref[:, span] = (rate * jnp.maximum(fitted, floor_ref[:, span])).astype(BF16)
    half_moments(1 - core_ref[0], basis_ref, value_ref, group_ref, out_ref, total_ref)


def keep_kernel(core_ref, basis_ref, value_ref, group_ref, out_ref, total_ref):
    half_moments(core_ref[0], basis_ref, value_ref, group_ref, out_ref, total_ref)


def inverse_kernel(near_ref, far_ref, out_ref, wide_ref):
    near = near_ref[...].reshape(PATHS // 2, LANES).astype(BF16)
    far = far_ref[...].reshape(PATHS // 2, LANES).astype(BF16)
    wide_ref[: PATHS // 2, :] = near
    wide_ref[PATHS // 2 :, :] = far
    gram = dot_tn(near, near) + dot_tn(far, far)
    row = lax.broadcasted_iota(jnp.int32, (K, K), 0)
    col = lax.broadcasted_iota(jnp.int32, (K, K), 1)
    eye = jnp.where(row == col, 1.0, 0.0).astype(F32)
    blocks = [
        [
            jnp.concatenate(
                [gram[d * K + i : d * K + i + 8, d * K : d * K + K], eye[i : i + 8]], axis=1
            )
            for i in range(0, K, 8)
        ]
        for d in range(DATES)
    ]
    below = lax.broadcasted_iota(jnp.int32, (8, LANES), 0)
    done = [[], []]
    for j in range(K):
        b, r = j // 8, j % 8
        for d in range(DATES):
            work = blocks[d]
            columns = [
                jnp.broadcast_to(work[i][:, j : j + 1], (8, LANES)) for i in range(b, K // 8)
            ]
            pivot = columns[0][r : r + 1, :]
            pivot_row = work[b][r : r + 1, :]
            done[d].append(pivot_row * lax.rsqrt(pivot))
            scaled = pivot_row / pivot
            for i in range(b, K // 8):
                factor = columns[i - b]
                if i == b:
                    factor = jnp.where(below > r, factor, 0.0)
                work[i] = work[i] - factor * scaled
    inverses = []
    for d in range(DATES):
        factor_inverse = jnp.concatenate(done[d], axis=0)[:, K:]
        inverses.append(dot_tn(factor_inverse, factor_inverse, HIGHEST))
    out_ref[...] = block_diagonal(*inverses)


def exposure_kernel(
    parts_ref, inverse_ref, basis_ref, wide_ref, exposure_ref, expected_ref
):
    peers = parts_ref.shape[0]
    halves = []
    for h in range(2):
        total = parts_ref[h]
        for i in range(h + 2, peers, 2):
            total = total + parts_ref[i]
        halves.append(total)
    moments = jnp.concatenate(halves, axis=0)
    beta = jnp.dot(moments, inverse_ref[...], precision=HIGHEST, preferred_element_type=F32)
    lane = lax.broadcasted_iota(jnp.int32, (SET_DEV, LANES), 1)
    rows = jnp.concatenate(
        [jnp.where(lane < K, beta, 0.0), jnp.where(lane < K, 0.0, beta)], axis=0
    )
    high, middle, low = split(rows)

    def smooth(basis):
        return dot_nt(basis, high) + dot_nt(basis, middle) + dot_nt(basis, low)

    mine = jnp.concatenate([basis_ref[0], basis_ref[1]], axis=1)
    exposure = jnp.maximum(smooth(mine), 0.0)
    exposure_ref[0] = exposure[:, :SET_DEV]
    exposure_ref[1] = exposure[:, SET_DEV:]
    total = jnp.zeros((8, LANES), F32)
    step = 512
    for i in range(PATHS // step):
        part = jnp.maximum(smooth(wide_ref[pl.ds(i * step, step), :]), 0.0)
        total = total + jnp.sum(part.reshape(step // 8, 8, LANES), axis=0)
    mean = jnp.sum(total, axis=0, keepdims=True) / PATHS
    expected_ref[0:1, :] = mean[:, :SET_DEV]
    expected_ref[1:2, :] = mean[:, SET_DEV:]


def params(**more):
    return pltpu.CompilerParams(vmem_limit_bytes=40 * 2**20, **more)


def shards(basis, fx_rates, coefficients, unwind_worth_minimum, position_offset_group, currency):
    paths = basis.shape[1]
    trades = coefficients.shape[1]
    core = lax.axis_index("core").reshape(1)
    swap = [(0, 1), (1, 0)]
    floor = unwind_worth_minimum.reshape(1, trades)
    group = position_offset_group.reshape(1, trades)
    names = currency.reshape(1, trades)

    flat = jnp.concatenate([basis[0], basis[1]], axis=1).astype(F32)
    near = lax.all_to_all(
        jnp.broadcast_to(flat[None], (lax.axis_size("z"), paths, LANES)), "z", 0, 0, tiled=True
    )

    moment_shape = jax.ShapeDtypeStruct((OWNERS, HALF, LANES), F32)
    total_scratch = pltpu.VMEM((OWNERS * HALF, DATES * paths), F32)
    send, value = pl.pallas_call(
        send_kernel,
        out_shape=(moment_shape, jax.ShapeDtypeStruct((DATES * paths, trades), BF16)),
        in_specs=[SMEM] + [VMEM] * 6,
        out_specs=(VMEM, VMEM),
        scratch_shapes=[total_scratch],
        compiler_params=params(),
        cost_estimate=pl.CostEstimate(
            flops=2 * 256 * 4096 * 1400, bytes_accessed=4 * 2**20, transcendentals=0
        ),
        name="values_and_sent_half",
    )(core, basis, fx_rates, coefficients, floor, group, names)
    received = lax.ppermute(send, "core", swap)
    kept = pl.pallas_call(
        keep_kernel,
        out_shape=moment_shape,
        in_specs=[SMEM] + [VMEM] * 3,
        out_specs=VMEM,
        scratch_shapes=[total_scratch],
        compiler_params=params(),
        cost_estimate=pl.CostEstimate(
            flops=2 * 256 * 4096 * 1024, bytes_accessed=3 * 2**20, transcendentals=0
        ),
        name="kept_half",
    )(core, basis, value, group)
    owned = lax.all_to_all(kept + received, ("x", "y"), 0, 0, tiled=True)

    far = lax.ppermute(near, "core", swap)
    inverse, wide = pl.pallas_call(
        inverse_kernel,
        out_shape=(
            jax.ShapeDtypeStruct((LANES, LANES), F32),
            jax.ShapeDtypeStruct((PATHS, LANES), BF16),
        ),
        in_specs=[VMEM] * 2,
        out_specs=(VMEM, VMEM),
        compiler_params=params(),
        cost_estimate=pl.CostEstimate(
            flops=2 * 2**31, bytes_accessed=2**21, transcendentals=0
        ),
        name="gram_inverse",
    )(near, far)

    summed = jnp.sum(owned, axis=0)
    peers = lax.axis_size("z") * lax.axis_size("core")
    parts = lax.all_to_all(
        jnp.broadcast_to(summed[None], (peers, HALF, LANES)), ("z", "core"), 0, 0, tiled=True
    )
    return pl.pallas_call(
        exposure_kernel,
        out_shape=(
            jax.ShapeDtypeStruct((DATES, paths, SET_DEV), F32),
            jax.ShapeDtypeStruct((DATES, SET_DEV), F32),
        ),
        in_specs=[VMEM] * 4,
        out_specs=(VMEM, VMEM),
        compiler_params=params(),
        name="exposure",
    )(parts, inverse, basis, wide)


def solution(mesh):
    parts = Mesh(mesh.devices.reshape(8, 2, 4, 8), ("z", "core", "x", "y"))
    path, trade = ("z", "core"), ("x", "y")
    return jax.shard_map(
        shards,
        mesh=parts,
        in_specs=(
            P(None, path, None),
            P(None, path, None),
            P(None, trade),
            P(trade),
            P(trade),
            P(trade),
        ),
        out_specs=(P(None, path, trade), P(None, trade)),
        check_vma=False,
    )
```

time: 430 us -> 77.7 us (0.18)
  the two profiles are of different devices: /device:TPU:4 before, /device:TPU:9 now
where the time goes in v1:
time: 77.7 us; the launch traced here: 77.1 us
  starting transfers between devices  31.5 us (41%)
  waiting for transfers between devices  23.4 us (30%)
  Pallas kernels  15.6 us (20%)
  local copies, waits for them, and re-layouts  4.86 us (6%)
  other arithmetic  0.93 us (1%)
    all_to_all x1, waiting for transfers between devices, shards(): owned = lax.all_to_all(kept + received, ('x', 'y'), 0, 0, tiled=True)  13.2 us
    all_to_all x1, starting transfers between devices, shards(): lax.all_to_all(jnp.broadcast_to(flat[None], (lax.axis_size('z'), paths, L...  10 us
    all_to_all x1, starting transfers between devices, shards(): owned = lax.all_to_all(kept + received, ('x', 'y'), 0, 0, tiled=True)  9.6 us
    pallas_call x1, Pallas kernels, shards(): pl.pallas_call(inverse_kernel, out_shape=(jax.ShapeDtypeStruct((LANES, LA...  6.08 us
    all_to_all x1, starting transfers between devices, shards(): lax.all_to_all(jnp.broadcast_to(summed[None], (peers, HALF, LANES)), ('z'...  6.04 us
    all_to_all x1, waiting for transfers between devices, shards(): lax.all_to_all(jnp.broadcast_to(summed[None], (peers, HALF, LANES)), ('z'...  5.76 us
    pallas_call x1, Pallas kernels, shards(): pl.pallas_call(send_kernel, out_shape=(moment_shape, jax.ShapeDtypeStruct...  4.52 us
    all_to_all x1, waiting for transfers between devices, shards(): lax.all_to_all(jnp.broadcast_to(flat[None], (lax.axis_size('z'), paths, L...  4.49 us
  transfers between devices with their start and end apart: 5, of which 3 were waited for; matrix products, arithmetic and copies ran while one was open for 4% of the time, Pallas kernels for 18%

profile of v1, /device:TPU:9, one launch (start us, length us, event | category | flops | bytes accessed | tf_op | source)
XLA Modules:
  0.0 77.1 jit_solution(12291511289223415624)
XLA Ops:
  0.6 0.0 copy-start.3
  0.6 0.0 copy-start.1
  0.7 0.0 copy-start.2
  0.7 0.0 copy-start
  0.7 0.8 %slice_bitcast_fusion.1 = (bf16[128,64]{0,1:T(8,128)(2,1)S(1)}, bf16[128,64]{0,1:T(8,128)(2,1)S(1)}) fusion(bf16[2,128,64]{1,2,0:T(8,128)(2,1)} %param.6), kind=kLoop, calls=%fused_computation.2 | loop fusion | bytes 65536 | tf_op jit(solution)/shard_map/concatenate | solution.py:198
  1.5 0.1 copy.11
  1.6 0.8 %broadcast_in_dim.5 = f32[8,128,128]{2,1,0:T(8,128)} broadcast(f32[128,128]{1,0:T(8,128)S(1)} %copy.11), dimensions={1,2} | broadcast | bytes 589824 | tf_op jit(solution)/shard_map/broadcast_in_dim | solution.py:200
  2.4 10.0 %all-to-all-start.2 = ((f32[8,128,128]{2,1,0:T(8,128)}), f32[8,128,128]{2,1,0:T(8,128)S(1)}, u32[]{:S(2)}, u32[]{:S(2)}) async-start(f32[8,128,128]{2,1,0:T(8,128)} %broadcast_in_dim.5), calls=%async_computation.2 | async-start | bytes 1048576 | tf_op jit(solution)/shard_map/all_to_all | solution.py:199
  12.4 0.9 %copy.10.basis_ref = bf16[2,128,64]{2,1,0:T(8,128)(2,1)S(1)} copy(bf16[2,128,64]{1,2,0:T(8,128)(2,1)} %param.6) | data formatting | bytes 65536 | tf_op args[0]
  13.3 0.8 %copy.9.fx_ref = f32[2,128,16]{2,1,0:T(8,128)S(1)} copy(f32[2,128,16]{1,2,0:T(8,128)} %param.7) | data formatting | bytes 32768 | tf_op args[1]
  14.1 0.0 copy-done.3
  14.1 0.0 copy-done.1
  14.2 0.0 copy-done.2
  14.2 0.0 copy-done
  14.2 4.5 %values_and_sent_half.1 = (f32[32,32,128]{2,1,0:T(8,128)S(1)}, bf16[256,4096]{1,0:T(8,128)(2,1)S(1)}) custom-call(s32[1]{0:T(128)} %bitcast.core_ref, bf16[2,128,64]{2,1,0:T(8,128)(2,1)S(1)} %copy.10.basis_ref, f32[2,128,16]{2,1,0:T(8,128)S(1)} %copy.9.fx_ref, bf16[64,4096]{1,0:T(8,128)(2,1)S(1)} %copy-done, f32[1,4096]{1,0:T(1,128)S(1)} %bitcast.8, ...), custom_call_target="tpu_custom_call" | custom-call | flops 2936012800 | bytes 4194304 | tf_op jit(solution)/shard_map/values_and_sent_half/pallas_call | solution.py:205
  18.7 2.9 %collective-permute-start = (f32[32,32,128]{2,1,0:T(8,128)S(1)}, f32[32,32,128]{2,1,0:T(8,128)S(1)}, u32[]{:S(2)}, u32[]{:S(2)}) collective-permute-start(f32[32,32,128]{2,1,0:T(8,128)S(1)} %get-tuple-element.7), channel_id=1, source_target_pairs={{0,32},{32,0},{1,33},{33,1},{2,34},{34,2},{3,35},{35,3},{4,36},{36... | collective-permute-start | bytes 1572872 | tf_op jit(solution)/shard_map/ppermute | solution.py:217
  21.6 3.4 %kept_half.1 = f32[32,32,128]{2,1,0:T(8,128)S(1)} custom-call(s32[1]{0:T(128)} %bitcast.core_ref, bf16[2,128,64]{2,1,0:T(8,128)(2,1)S(1)} %copy.10.basis_ref, bf16[256,4096]{1,0:T(8,128)(2,1)S(1)} %get-tuple-element.6.value_ref, s32[1,4096]{1,0:T(1,128)S(1)} %bitcast.11), custom_call_target="tpu_custom_call" | custom-call | flops 2147483648 | bytes 3145728 | tf_op jit(solution)/shard_map/kept_half/pallas_call | solution.py:218
  25.0 0.0 collective-permute-done
  25.0 0.9 %add.3 = f32[32,32,128]{2,1,0:T(8,128)} add(f32[32,32,128]{2,1,0:T(8,128)S(1)} %kept_half.1, f32[32,32,128]{2,1,0:T(8,128)S(1)} %collective-permute-done) | non-fusion elementwise | flops 131072 | bytes 1572864 | tf_op jit(solution)/shard_map/add | solution.py:230
  25.9 4.5 %all-to-all-done.2.near_ref = f32[8,128,128]{2,1,0:T(8,128)S(1)} async-done(((f32[8,128,128]{2,1,0:T(8,128)}), f32[8,128,128]{2,1,0:T(8,128)S(1)}, u32[]{:S(2)}, u32[]{:S(2)}) %all-to-all-start.2) | async-done | bytes 524320 | tf_op jit(solution)/shard_map/all_to_all | solution.py:199
  30.4 9.6 %all-to-all-start = ((f32[32,32,128]{2,1,0:T(8,128)}), f32[32,32,128]{2,1,0:T(8,128)S(1)}, u32[]{:S(2)}, u32[]{:S(2)}) async-start(f32[32,32,128]{2,1,0:T(8,128)} %add.3), calls=%async_computation | async-start | bytes 1048576 | tf_op jit(solution)/shard_map/all_to_all | solution.py:230
  40.0 3.0 %collective-permute-start.1 = (f32[8,128,128]{2,1,0:T(8,128)S(1)}, f32[8,128,128]{2,1,0:T(8,128)S(1)}, u32[]{:S(2)}, u32[]{:S(2)}) collective-permute-start(f32[8,128,128]{2,1,0:T(8,128)S(1)} %all-to-all-done.2.near_ref), channel_id=1, source_target_pairs={{0,32},{32,0},{1,33},{33,1},{2,34},{34,2},{3,35},{35,3},{4,36},{36... | collective-permute-start | bytes 1572872 | tf_op jit(solution)/shard_map/ppermute | solution.py:232
  43.0 13.2 %all-to-all-done = f32[32,32,128]{2,1,0:T(8,128)S(1)} async-done(((f32[32,32,128]{2,1,0:T(8,128)}), f32[32,32,128]{2,1,0:T(8,128)S(1)}, u32[]{:S(2)}, u32[]{:S(2)}) %all-to-all-start) | async-done | bytes 524320 | tf_op jit(solution)/shard_map/all_to_all | solution.py:230
  56.2 0.7 broadcast_in_dim.4
  56.9 6.0 %all-to-all-start.1 = ((f32[16,32,128]{2,1,0:T(8,128)}), f32[16,32,128]{2,1,0:T(8,128)S(1)}, u32[]{:S(2)}, u32[]{:S(2)}) async-start(f32[16,32,128]{2,1,0:T(8,128)} %broadcast_in_dim.4), calls=%async_computation.1 | async-start | bytes 524288 | tf_op jit(solution)/shard_map/all_to_all | solution.py:250
  63.0 0.0 collective-permute-done.1.far_ref
  63.0 6.1 %gram_inverse.1 = (f32[128,128]{1,0:T(8,128)S(1)}, bf16[2048,128]{1,0:T(8,128)(2,1)S(1)}) custom-call(f32[8,128,128]{2,1,0:T(8,128)S(1)} %all-to-all-done.2.near_ref, f32[8,128,128]{2,1,0:T(8,128)S(1)} %collective-permute-done.1.far_ref), custom_call_target="tpu_custom_call" | custom-call | flops 4294967296 | bytes 2097152 | tf_op jit(solution)/shard_map/gram_inverse/pallas_call | solution.py:233
  69.1 5.8 %all-to-all-done.1.parts_ref = f32[16,32,128]{2,1,0:T(8,128)S(1)} async-done(((f32[16,32,128]{2,1,0:T(8,128)}), f32[16,32,128]{2,1,0:T(8,128)S(1)}, u32[]{:S(2)}, u32[]{:S(2)}) %all-to-all-start.1) | async-done | bytes 262176 | tf_op jit(solution)/shard_map/all_to_all | solution.py:250
  74.8 1.5 %exposure.1 = (f32[2,128,64]{2,1,0:T(8,128)S(1)}, f32[2,64]{1,0:T(2,128)}) custom-call(f32[16,32,128]{2,1,0:T(8,128)S(1)} %all-to-all-done.1.parts_ref, f32[128,128]{1,0:T(8,128)S(1)} %get-tuple-element.8.inverse_ref, bf16[2,128,64]{2,1,0:T(8,128)(2,1)S(1)} %copy.10.basis_ref, bf16[2048,128]{1,0:T(8,128)(2,1)S(1)} %get-tuple-element.9.wide_ref), custom_call_target="tpu_custom_call" | custom-call | tf_op jit(solution)/shard_map/exposure/pallas_call | solution.py:253
  76.4 0.7 copy.13
  (2 shorter events, 0.1 us)
Async XLA Ops:
  0.6 13.5 %copy-start.3 = (s32[4096]{0:T(1024)S(1)}, s32[4096]{0:T(1024)}, u32[]{:S(2)}) copy-start(s32[4096]{0:T(1024)} %param.10) | copy-start | bytes 49156
  0.6 13.5 %copy-start.1 = (f32[4096]{0:T(1024)S(1)}, f32[4096]{0:T(1024)}, u32[]{:S(2)}) copy-start(f32[4096]{0:T(1024)} %param.9) | copy-start | bytes 49156
  0.7 13.5 %copy-start.2 = (s32[4096]{0:T(1024)S(1)}, s32[4096]{0:T(1024)}, u32[]{:S(2)}) copy-start(s32[4096]{0:T(1024)} %param.11) | copy-start | bytes 49156
  0.7 13.5 %copy-start = (bf16[64,4096]{1,0:T(8,128)(2,1)S(1)}, bf16[64,4096]{1,0:T(8,128)(2,1)}, u32[]{:S(2)}) copy-start(bf16[64,4096]{1,0:T(8,128)(2,1)} %coef_ref.1) | copy-start | bytes 1572868
  2.4 28.0 %all-to-all-start.2 = ((f32[8,128,128]{2,1,0:T(8,128)}), f32[8,128,128]{2,1,0:T(8,128)S(1)}, u32[]{:S(2)}, u32[]{:S(2)}) async-start(f32[8,128,128]{2,1,0:T(8,128)} %broadcast_in_dim.5), calls=%async_computation.2 | async-start | bytes 1048576 | tf_op jit(solution)/shard_map/all_to_all | solution.py:199
  18.7 6.3 %collective-permute-start = (f32[32,32,128]{2,1,0:T(8,128)S(1)}, f32[32,32,128]{2,1,0:T(8,128)S(1)}, u32[]{:S(2)}, u32[]{:S(2)}) collective-permute-start(f32[32,32,128]{2,1,0:T(8,128)S(1)} %get-tuple-element.7), channel_id=1, source_target_pairs={{0,32},{32,0},{1,33},{33,1},{2,34},{34,2},{3,35},{35,3},{4,36},{36... | collective-permute-start | bytes 1572872 | tf_op jit(solution)/shard_map/ppermute | solution.py:217
  30.4 25.8 %all-to-all-start = ((f32[32,32,128]{2,1,0:T(8,128)}), f32[32,32,128]{2,1,0:T(8,128)S(1)}, u32[]{:S(2)}, u32[]{:S(2)}) async-start(f32[32,32,128]{2,1,0:T(8,128)} %add.3), calls=%async_computation | async-start | bytes 1048576 | tf_op jit(solution)/shard_map/all_to_all | solution.py:230
  40.0 23.0 %collective-permute-start.1 = (f32[8,128,128]{2,1,0:T(8,128)S(1)}, f32[8,128,128]{2,1,0:T(8,128)S(1)}, u32[]{:S(2)}, u32[]{:S(2)}) collective-permute-start(f32[8,128,128]{2,1,0:T(8,128)S(1)} %all-to-all-done.2.near_ref), channel_id=1, source_target_pairs={{0,32},{32,0},{1,33},{33,1},{2,34},{34,2},{3,35},{35,3},{4,36},{36... | collective-permute-start | bytes 1572872 | tf_op jit(solution)/shard_map/ppermute | solution.py:232
  56.9 17.9 %all-to-all-start.1 = ((f32[16,32,128]{2,1,0:T(8,128)}), f32[16,32,128]{2,1,0:T(8,128)S(1)}, u32[]{:S(2)}, u32[]{:S(2)}) async-start(f32[16,32,128]{2,1,0:T(8,128)} %broadcast_in_dim.4), calls=%async_computation.1 | async-start | bytes 524288 | tf_op jit(solution)/shard_map/all_to_all | solution.py:250

commit v2 on v1

--- a/solution.py
+++ b/solution.py
@@ -52,7 +52,7 @@
     )
 
 
-def half_moments(half, basis_ref, value_ref, group_ref, out_ref, total_ref):
+def half_moments(half, wide, value_ref, group_ref, out_ref, total_ref):
     rows = OWNERS * HALF
     trades = value_ref.shape[1]
     for i in range(trades // TILE):
@@ -67,7 +67,6 @@
             total_ref[...] = part
         else:
             total_ref[...] += part
-    wide = block_diagonal(basis_ref[0], basis_ref[1])
     step = 256
     for i in range(rows // step):
         span = pl.ds(i * step, step)
@@ -82,14 +81,19 @@
         )
 
 
+def by_path(basis_ref):
+    return [basis_ref[d].astype(F32).T.astype(BF16) for d in range(DATES)]
+
+
 def send_kernel(
     core_ref, basis_ref, fx_ref, coef_ref, floor_ref, group_ref, currency_ref,
     out_ref, value_ref, total_ref,
 ):
-    paths = basis_ref.shape[1]
     trades = coef_ref.shape[1]
-    basis = basis_ref[...].reshape(DATES * paths, K)
-    rates = jnp.concatenate(split(fx_ref[...].reshape(DATES * paths, NF)), axis=1)
+    parts = by_path(basis_ref)
+    basis = jnp.concatenate(parts, axis=0)
+    fx = jnp.concatenate([fx_ref[d].T for d in range(DATES)], axis=0)
+    rates = jnp.concatenate(split(fx), axis=1)
     for i in range(trades // TILE):
         span = pl.ds(i * TILE, TILE)
         fitted = jnp.dot(basis, coef_ref[:, span], preferred_element_type=F32)
@@ -97,52 +101,66 @@
         chosen = jnp.where(names == currency_ref[:, span], 1.0, 0.0).astype(BF16)
         rate = jnp.dot(rates, chosen, preferred_element_type=F32)
         value_ref[:, span] = (rate * jnp.maximum(fitted, floor_ref[:, span])).astype(BF16)
-    half_moments(1 - core_ref[0], basis_ref, value_ref, group_ref, out_ref, total_ref)
+    wide = block_diagonal(*parts)
+    half_moments(1 - core_ref[0], wide, value_ref, group_ref, out_ref, total_ref)
 
 
 def keep_kernel(core_ref, basis_ref, value_ref, group_ref, out_ref, total_ref):
-    half_moments(core_ref[0], basis_ref, value_ref, group_ref, out_ref, total_ref)
+    wide = block_diagonal(*by_path(basis_ref))
+    half_moments(core_ref[0], wide, value_ref, group_ref, out_ref, total_ref)
+
+
+def eliminate(blocks):
+    row = lax.broadcasted_iota(jnp.int32, (8, LANES), 0)
+    done = []
+    for b in range(K // 8):
+        height = K // 8 - b
+        columns = [
+            [
+                jnp.broadcast_to(blocks[i][:, b * 8 + c : b * 8 + c + 1], (8, LANES))
+                for i in range(b, K // 8)
+            ]
+            for c in range(8)
+        ]
+        rows = [blocks[b][c : c + 1, :] for c in range(8)]
+        for c in range(8):
+            pivot = columns[c][0][c : c + 1, :]
+            inverse = 1.0 / pivot
+            done.append(rows[c] * lax.rsqrt(pivot))
+            scaled = rows[c] * inverse
+            for e in range(c + 1, 8):
+                entry = columns[c][0][e : e + 1, :]
+                rows[e] = rows[e] - entry * scaled
+                ratio = entry * inverse
+                for i in range(height):
+                    columns[e][i] = columns[e][i] - columns[c][i] * ratio
+            for i in range(1, height):
+                blocks[b + i] = blocks[b + i] - columns[c][i] * scaled
+    return jnp.concatenate(done, axis=0)
 
 
 def inverse_kernel(near_ref, far_ref, out_ref, wide_ref):
-    near = near_ref[...].reshape(PATHS // 2, LANES).astype(BF16)
-    far = far_ref[...].reshape(PATHS // 2, LANES).astype(BF16)
-    wide_ref[: PATHS // 2, :] = near
-    wide_ref[PATHS // 2 :, :] = far
-    gram = dot_tn(near, near) + dot_tn(far, far)
+    groups = near_ref.shape[0]
+    paths = near_ref.shape[2]
+    gram = jnp.zeros((LANES, LANES), F32)
+    for i, ref in enumerate((near_ref, far_ref)):
+        for z in range(groups):
+            at = (i * groups + z) * paths
+            wide_ref[:, at : at + paths] = ref[z].astype(BF16)
+    every = wide_ref[...]
+    gram = dot_nt(every, every)
     row = lax.broadcasted_iota(jnp.int32, (K, K), 0)
     col = lax.broadcasted_iota(jnp.int32, (K, K), 1)
     eye = jnp.where(row == col, 1.0, 0.0).astype(F32)
-    blocks = [
-        [
+    inverses = []
+    for d in range(DATES):
+        blocks = [
             jnp.concatenate(
                 [gram[d * K + i : d * K + i + 8, d * K : d * K + K], eye[i : i + 8]], axis=1
             )
             for i in range(0, K, 8)
         ]
-        for d in range(DATES)
-    ]
-    below = lax.broadcasted_iota(jnp.int32, (8, LANES), 0)
-    done = [[], []]
-    for j in range(K):
-        b, r = j // 8, j % 8
-        for d in range(DATES):
-            work = blocks[d]
-            columns = [
-                jnp.broadcast_to(work[i][:, j : j + 1], (8, LANES)) for i in range(b, K // 8)
-            ]
-            pivot = columns[0][r : r + 1, :]
-            pivot_row = work[b][r : r + 1, :]
-            done[d].append(pivot_row * lax.rsqrt(pivot))
-            scaled = pivot_row / pivot
-            for i in range(b, K // 8):
-                factor = columns[i - b]
-                if i == b:
-                    factor = jnp.where(below > r, factor, 0.0)
-                work[i] = work[i] - factor * scaled
-    inverses = []
-    for d in range(DATES):
-        factor_inverse = jnp.concatenate(done[d], axis=0)[:, K:]
+        factor_inverse = eliminate(blocks)[:, K:]
         inverses.append(dot_tn(factor_inverse, factor_inverse, HIGHEST))
     out_ref[...] = block_diagonal(*inverses)
 
@@ -163,21 +181,24 @@
     rows = jnp.concatenate(
         [jnp.where(lane < K, beta, 0.0), jnp.where(lane < K, 0.0, beta)], axis=0
     )
-    high, middle, low = split(rows)
-
-    def smooth(basis):
-        return dot_nt(basis, high) + dot_nt(basis, middle) + dot_nt(basis, low)
-
-    mine = jnp.concatenate([basis_ref[0], basis_ref[1]], axis=1)
-    exposure = jnp.maximum(smooth(mine), 0.0)
-    exposure_ref[0] = exposure[:, :SET_DEV]
-    exposure_ref[1] = exposure[:, SET_DEV:]
-    total = jnp.zeros((8, LANES), F32)
+    stacked = jnp.concatenate(split(rows), axis=0)
+
+    def exposed(basis):
+        smooth = jnp.dot(stacked, basis, preferred_element_type=F32)
+        return jnp.maximum(
+            smooth[:LANES] + smooth[LANES : 2 * LANES] + smooth[2 * LANES :], 0.0
+        )
+
+    paths = basis_ref.shape[2]
+    exposure = exposed(basis_ref[...].reshape(LANES, paths))
+    exposure_ref[...] = exposure.reshape(DATES, SET_DEV, paths)
+    total = jnp.zeros((LANES, 128), F32)
     step = 512
     for i in range(PATHS // step):
-        part = jnp.maximum(smooth(wide_ref[pl.ds(i * step, step), :]), 0.0)
-        total = total + jnp.sum(part.reshape(step // 8, 8, LANES), axis=0)
-    mean = jnp.sum(total, axis=0, keepdims=True) / PATHS
+        part = exposed(wide_ref[:, i * step : (i + 1) * step])
+        for j in range(step // 128):
+            total = total + part[:, j * 128 : (j + 1) * 128]
+    mean = jnp.sum(total.T, axis=0, keepdims=True) / PATHS
     expected_ref[0:1, :] = mean[:, :SET_DEV]
     expected_ref[1:2, :] = mean[:, SET_DEV:]
 
@@ -194,11 +215,9 @@
     floor = unwind_worth_minimum.reshape(1, trades)
     group = position_offset_group.reshape(1, trades)
     names = currency.reshape(1, trades)
-
-    flat = jnp.concatenate([basis[0], basis[1]], axis=1).astype(F32)
-    near = lax.all_to_all(
-        jnp.broadcast_to(flat[None], (lax.axis_size("z"), paths, LANES)), "z", 0, 0, tiled=True
-    )
+    basis = jnp.swapaxes(basis, 1, 2)
+    fx_rates = jnp.swapaxes(fx_rates, 1, 2)
+    flat = basis.reshape(LANES, paths).astype(F32)
 
     moment_shape = jax.ShapeDtypeStruct((OWNERS, HALF, LANES), F32)
     total_scratch = pltpu.VMEM((OWNERS * HALF, DATES * paths), F32)
@@ -227,14 +246,20 @@
         ),
         name="kept_half",
     )(core, basis, value, group)
-    owned = lax.all_to_all(kept + received, ("x", "y"), 0, 0, tiled=True)
+    pair = kept + received
+
+    flat, pair = lax.optimization_barrier((flat, pair))
+    owned = lax.all_to_all(pair, ("x", "y"), 0, 0, tiled=True)
+    near = lax.all_to_all(
+        jnp.broadcast_to(flat[None], (lax.axis_size("z"), LANES, paths)), "z", 0, 0, tiled=True
+    )
 
     far = lax.ppermute(near, "core", swap)
     inverse, wide = pl.pallas_call(
         inverse_kernel,
         out_shape=(
             jax.ShapeDtypeStruct((LANES, LANES), F32),
-            jax.ShapeDtypeStruct((PATHS, LANES), BF16),
+            jax.ShapeDtypeStruct((LANES, PATHS), BF16),
         ),
         in_specs=[VMEM] * 2,
         out_specs=(VMEM, VMEM),
@@ -250,10 +275,10 @@
     parts = lax.all_to_all(
         jnp.broadcast_to(summed[None], (peers, HALF, LANES)), ("z", "core"), 0, 0, tiled=True
     )
-    return pl.pallas_call(
+    exposure, expected = pl.pallas_call(
         exposure_kernel,
         out_shape=(
-            jax.ShapeDtypeStruct((DATES, paths, SET_DEV), F32),
+            jax.ShapeDtypeStruct((DATES, SET_DEV, paths), F32),
             jax.ShapeDtypeStruct((DATES, SET_DEV), F32),
         ),
         in_specs=[VMEM] * 4,
@@ -261,6 +286,7 @@
         compiler_params=params(),
         name="exposure",
     )(parts, inverse, basis, wide)
+    return jnp.swapaxes(exposure, 1, 2), expected
 
 
 def solution(mesh):

time: 77.7 us -> 91.6 us (1.18)
  blocking collectives: 0 us -> 27.8 us
  starting transfers between devices: 31.5 us -> 21.1 us
  Pallas kernels: 15.6 us -> 12.3 us
  waiting for transfers between devices: 23.4 us -> 22.4 us
    all_to_all x0 -> x1, blocking collectives: none -> 27.8 us  [shards(): lax.all_to_all(jnp.broadcast_to(flat[None], (lax.axis_size('z'), LANES, p...]
    all_to_all x2 -> x1, starting transfers between devices: 19.6 us -> 9.6 us  [shards(): owned = lax.all_to_all(pair, ('x', 'y'), 0, 0, tiled=True)]
    all_to_all x2 -> x1, waiting for transfers between devices: 17.7 us -> 13.2 us  [shards(): owned = lax.all_to_all(pair, ('x', 'y'), 0, 0, tiled=True)]
    pallas_call x1, Pallas kernels: 6.08 us -> 2.66 us  [shards(): pl.pallas_call(inverse_kernel, out_shape=(jax.ShapeDtypeStruct((LANES, LA...]
    all_to_all x1, waiting for transfers between devices: 5.76 us -> 9.18 us  [shards(): lax.all_to_all(jnp.broadcast_to(summed[None], (peers, HALF, LANES)), ('z'...]
    unnamed x10 -> x16, local copies, waits for them, and re-layouts: 1.7 us -> 4.67 us
  transfers between devices with their start and end apart: 5 -> 4, of which waited for: 3 -> 2; matrix products, arithmetic and copies ran while one was open for 4% -> 1% of each run, Pallas kernels for 18% -> 7%
where the time goes in v2:
time: 91.6 us; the launch traced here: 90.8 us
  blocking collectives  27.8 us (30%)
  waiting for transfers between devices  22.4 us (24%)
  starting transfers between devices  21.1 us (23%)
  Pallas kernels  12.3 us (13%)
  local copies, waits for them, and re-layouts  5.44 us (6%)
  other arithmetic  0.93 us (1%)
    all_to_all x1, blocking collectives, shards(): lax.all_to_all(jnp.broadcast_to(flat[None], (lax.axis_size('z'), LANES, p...  27.8 us
    all_to_all x1, waiting for transfers between devices, shards(): owned = lax.all_to_all(pair, ('x', 'y'), 0, 0, tiled=True)  13.2 us
    all_to_all x1, starting transfers between devices, shards(): owned = lax.all_to_all(pair, ('x', 'y'), 0, 0, tiled=True)  9.6 us
    all_to_all x1, waiting for transfers between devices, shards(): lax.all_to_all(jnp.broadcast_to(summed[None], (peers, HALF, LANES)), ('z'...  9.18 us
    all_to_all x1, starting transfers between devices, shards(): lax.all_to_all(jnp.broadcast_to(summed[None], (peers, HALF, LANES)), ('z'...  6.01 us
    unnamed x16, local copies, waits for them, and re-layouts  4.67 us
    pallas_call x1, Pallas kernels, shards(): pl.pallas_call(send_kernel, out_shape=(moment_shape, jax.ShapeDtypeStruct...  4.67 us
    pallas_call x1, Pallas kernels, shards(): pl.pallas_call(keep_kernel, out_shape=moment_shape, in_specs=[SMEM] + [VM...  3.45 us
  transfers between devices with their start and end apart: 4, of which 2 were waited for; matrix products, arithmetic and copies ran while one was open for 1% of the time, Pallas kernels for 7%

profile of v2, /device:TPU:9, one launch (start us, length us, event | category | flops | bytes accessed | tf_op | source)
XLA Modules:
  0.0 90.8 jit_solution(4667478093036603801)
XLA Ops:
  0.6 0.0 copy-start
  0.6 0.7 copy-done
  1.4 0.0 copy-start.2
  1.4 1.0 %copy-done.2 = bf16[64,4096]{1,0:T(8,128)(2,1)S(1)} copy-done((bf16[64,4096]{1,0:T(8,128)(2,1)S(1)}, bf16[64,4096]{1,0:T(8,128)(2,1)}, u32[]{:S(2)}) %copy-start.2) | copy-done | bytes 524312
  2.4 0.0 copy-start.3
  2.4 0.7 copy-done.3
  3.2 0.0 copy-start.4
  3.2 0.7 copy-done.4
  3.9 0.0 copy-start.5
  3.9 0.7 copy-done.5
  4.6 0.0 copy-start.6
  4.6 0.7 copy-done.6
  5.3 0.0 copy-start.7
  5.3 4.7 %values_and_sent_half.1 = (f32[32,32,128]{2,1,0:T(8,128)S(1)}, bf16[256,4096]{1,0:T(8,128)(2,1)S(1)}) custom-call(s32[1]{0:T(128)} %bitcast.2.core_ref, bf16[2,64,128]{2,1,0:T(8,128)(2,1)S(1)} %bitcast.11, f32[2,16,128]{2,1,0:T(8,128)S(1)} %bitcast.14, bf16[64,4096]{1,0:T(8,128)(2,1)S(1)} %copy-done.2, f32[1,4096]{1,0:T(1,128)S(1)} %bitcast.15, ...), custom_call_target="tpu_custom_call" | custom-call | flops 2936012800 | bytes 4194304 | tf_op jit(solution)/shard_map/values_and_sent_half/pallas_call | solution.py:224
  10.0 2.6 %collective-permute-start = (f32[32,32,128]{2,1,0:T(8,128)S(1)}, f32[32,32,128]{2,1,0:T(8,128)S(1)}, u32[]{:S(2)}, u32[]{:S(2)}) collective-permute-start(f32[32,32,128]{2,1,0:T(8,128)S(1)} %get-tuple-element.11), channel_id=1, source_target_pairs={{0,32},{32,0},{1,33},{33,1},{2,34},{34,2},{3,35},{35,3},{4,36},{36... | collective-permute-start | bytes 1572872 | tf_op jit(solution)/shard_map/ppermute | solution.py:236
  12.6 0.0 copy-done.7
  12.6 3.4 %kept_half.1 = f32[32,32,128]{2,1,0:T(8,128)S(1)} custom-call(s32[1]{0:T(128)} %bitcast.2.core_ref, bf16[2,64,128]{2,1,0:T(8,128)(2,1)S(1)} %bitcast.12, bf16[256,4096]{1,0:T(8,128)(2,1)S(1)} %get-tuple-element.10.value_ref, s32[1,4096]{1,0:T(1,128)S(1)} %bitcast.18), custom_call_target="tpu_custom_call" | custom-call | flops 2147483648 | bytes 3145728 | tf_op jit(solution)/shard_map/kept_half/pallas_call | solution.py:237
  16.1 0.0 collective-permute-done
  16.1 0.9 add.3
  17.0 27.8 %all_to_all.15.near_ref = f32[8,128,128]{2,1,0:T(8,128)S(1)} all-to-all(f32[8,128,128]{2,1,0:T(8,128)S(1)} %broadcast_in_dim.5), channel_id=1, replica_groups=mesh['z'=8,'core'=2,'x'=4,'y'=8] {'z'}, dimensions={0} | all-to-all | bytes 1048576 | tf_op jit(solution)/shard_map/all_to_all | solution.py:253
  44.8 9.6 %all-to-all-start = ((f32[32,32,128]{2,1,0:T(8,128)}), f32[32,32,128]{2,1,0:T(8,128)S(1)}, u32[]{:S(2)}, u32[]{:S(2)}) async-start(f32[32,32,128]{2,1,0:T(8,128)} %add.3), calls=%async_computation | async-start | bytes 1048576 | tf_op jit(solution)/shard_map/all_to_all | solution.py:252
  54.4 2.9 %collective-permute-start.1 = (f32[8,128,128]{2,1,0:T(8,128)S(1)}, f32[8,128,128]{2,1,0:T(8,128)S(1)}, u32[]{:S(2)}, u32[]{:S(2)}) collective-permute-start(f32[8,128,128]{2,1,0:T(8,128)S(1)} %all_to_all.15.near_ref), channel_id=1, source_target_pairs={{0,32},{32,0},{1,33},{33,1},{2,34},{34,2},{3,35},{35,3},{4,36},{36... | collective-permute-start | bytes 1572872 | tf_op jit(solution)/shard_map/ppermute | solution.py:257
  57.3 13.2 %all-to-all-done = f32[32,32,128]{2,1,0:T(8,128)S(1)} async-done(((f32[32,32,128]{2,1,0:T(8,128)}), f32[32,32,128]{2,1,0:T(8,128)S(1)}, u32[]{:S(2)}, u32[]{:S(2)}) %all-to-all-start) | async-done | bytes 524320 | tf_op jit(solution)/shard_map/all_to_all | solution.py:252
  70.6 0.7 broadcast_in_dim.4
  71.4 6.0 %all-to-all-start.1 = ((f32[16,32,128]{2,1,0:T(8,128)}), f32[16,32,128]{2,1,0:T(8,128)S(1)}, u32[]{:S(2)}, u32[]{:S(2)}) async-start(f32[16,32,128]{2,1,0:T(8,128)} %broadcast_in_dim.4), calls=%async_computation.1 | async-start | bytes 524288 | tf_op jit(solution)/shard_map/all_to_all | solution.py:275
  77.4 0.0 copy-start.1
  77.4 0.0 collective-permute-done.1.far_ref
  77.4 2.7 %gram_inverse.1 = (f32[128,128]{1,0:T(8,128)S(1)}, bf16[128,2048]{1,0:T(8,128)(2,1)S(1)}) custom-call(f32[8,128,128]{2,1,0:T(8,128)S(1)} %all_to_all.15.near_ref, f32[8,128,128]{2,1,0:T(8,128)S(1)} %collective-permute-done.1.far_ref), custom_call_target="tpu_custom_call" | custom-call | flops 4294967296 | bytes 2097152 | tf_op jit(solution)/shard_map/gram_inverse/pallas_call | solution.py:258
  80.1 9.2 %all-to-all-done.1.parts_ref = f32[16,32,128]{2,1,0:T(8,128)S(1)} async-done(((f32[16,32,128]{2,1,0:T(8,128)}), f32[16,32,128]{2,1,0:T(8,128)S(1)}, u32[]{:S(2)}, u32[]{:S(2)}) %all-to-all-start.1) | async-done | bytes 262176 | tf_op jit(solution)/shard_map/all_to_all | solution.py:275
  89.2 0.0 copy-done.1
  89.2 1.6 %exposure.1 = (f32[2,64,128]{2,1,0:T(8,128)}, f32[2,64]{1,0:T(2,128)}) custom-call(f32[16,32,128]{2,1,0:T(8,128)S(1)} %all-to-all-done.1.parts_ref, f32[128,128]{1,0:T(8,128)S(1)} %get-tuple-element.14.inverse_ref, bf16[2,64,128]{2,1,0:T(8,128)(2,1)S(1)} %bitcast.13, bf16[128,2048]{1,0:T(8,128)(2,1)S(1)} %get-tuple-element.15.wide_ref), custom_call_target="tpu_custom_call" | custom-call | tf_op jit(solution)/shard_map/exposure/pallas_call | solution.py:278
  (3 shorter events, 0.1 us)
Async XLA Ops:
  0.6 0.8 copy-start
  1.4 1.0 %copy-start.2 = (bf16[64,4096]{1,0:T(8,128)(2,1)S(1)}, bf16[64,4096]{1,0:T(8,128)(2,1)}, u32[]{:S(2)}) copy-start(bf16[64,4096]{1,0:T(8,128)(2,1)} %coef_ref.1) | copy-start | bytes 1572868
  2.4 0.7 copy-start.3
  3.2 0.7 copy-start.4
  3.9 0.7 copy-start.5
  4.6 0.7 copy-start.6
  5.3 7.3 %copy-start.7 = (s32[4096]{0:T(1024)S(1)}, s32[4096]{0:T(1024)}, u32[]{:S(2)}) copy-start(s32[4096]{0:T(1024)} %param.10) | copy-start | bytes 49156
  10.0 6.1 %collective-permute-start = (f32[32,32,128]{2,1,0:T(8,128)S(1)}, f32[32,32,128]{2,1,0:T(8,128)S(1)}, u32[]{:S(2)}, u32[]{:S(2)}) collective-permute-start(f32[32,32,128]{2,1,0:T(8,128)S(1)} %get-tuple-element.11), channel_id=1, source_target_pairs={{0,32},{32,0},{1,33},{33,1},{2,34},{34,2},{3,35},{35,3},{4,36},{36... | collective-permute-start | bytes 1572872 | tf_op jit(solution)/shard_map/ppermute | solution.py:236
  44.8 25.8 %all-to-all-start = ((f32[32,32,128]{2,1,0:T(8,128)}), f32[32,32,128]{2,1,0:T(8,128)S(1)}, u32[]{:S(2)}, u32[]{:S(2)}) async-start(f32[32,32,128]{2,1,0:T(8,128)} %add.3), calls=%async_computation | async-start | bytes 1048576 | tf_op jit(solution)/shard_map/all_to_all | solution.py:252
  54.4 23.0 %collective-permute-start.1 = (f32[8,128,128]{2,1,0:T(8,128)S(1)}, f32[8,128,128]{2,1,0:T(8,128)S(1)}, u32[]{:S(2)}, u32[]{:S(2)}) collective-permute-start(f32[8,128,128]{2,1,0:T(8,128)S(1)} %all_to_all.15.near_ref), channel_id=1, source_target_pairs={{0,32},{32,0},{1,33},{33,1},{2,34},{34,2},{3,35},{35,3},{4,36},{36... | collective-permute-start | bytes 1572872 | tf_op jit(solution)/shard_map/ppermute | solution.py:257
  71.4 17.9 %all-to-all-start.1 = ((f32[16,32,128]{2,1,0:T(8,128)}), f32[16,32,128]{2,1,0:T(8,128)S(1)}, u32[]{:S(2)}, u32[]{:S(2)}) async-start(f32[16,32,128]{2,1,0:T(8,128)} %broadcast_in_dim.4), calls=%async_computation.1 | async-start | bytes 524288 | tf_op jit(solution)/shard_map/all_to_all | solution.py:275
  77.4 11.9 %copy-start.1 = (bf16[2,128,64]{1,2,0:T(8,128)(2,1)S(1)}, bf16[2,128,64]{1,2,0:T(8,128)(2,1)}, u32[]{:S(2)}) copy-start(bf16[2,128,64]{1,2,0:T(8,128)(2,1)} %param.6) | copy-start | bytes 98308

commit v3 on v2

--- a/solution.py
+++ b/solution.py
@@ -219,6 +219,10 @@
     fx_rates = jnp.swapaxes(fx_rates, 1, 2)
     flat = basis.reshape(LANES, paths).astype(F32)
 
+    near = lax.all_to_all(
+        jnp.broadcast_to(flat[None], (lax.axis_size("z"), LANES, paths)), "z", 0, 0, tiled=True
+    )
+
     moment_shape = jax.ShapeDtypeStruct((OWNERS, HALF, LANES), F32)
     total_scratch = pltpu.VMEM((OWNERS * HALF, DATES * paths), F32)
     send, value = pl.pallas_call(
@@ -247,12 +251,7 @@
         name="kept_half",
     )(core, basis, value, group)
     pair = kept + received
-
-    flat, pair = lax.optimization_barrier((flat, pair))
     owned = lax.all_to_all(pair, ("x", "y"), 0, 0, tiled=True)
-    near = lax.all_to_all(
-        jnp.broadcast_to(flat[None], (lax.axis_size("z"), LANES, paths)), "z", 0, 0, tiled=True
-    )
 
     far = lax.ppermute(near, "core", swap)
     inverse, wide = pl.pallas_call(
@@ -271,6 +270,7 @@
     )(near, far)
 
     summed = jnp.sum(owned, axis=0)
+    inverse, summed = lax.optimization_barrier((inverse, summed))
     peers = lax.axis_size("z") * lax.axis_size("core")
     parts = lax.all_to_all(
         jnp.broadcast_to(summed[None], (peers, HALF, LANES)), ("z", "core"), 0, 0, tiled=True

time: 91.6 us -> 78.5 us (0.86)
  waiting for transfers between devices: 22.4 us -> 11.9 us
  blocking collectives: 27.8 us -> 20.1 us
  starting transfers between devices: 21.1 us -> 25.5 us
    all_to_all x1, waiting for transfers between devices: 9.18 us -> 1.39 us  [shards(): lax.all_to_all(jnp.broadcast_to(flat[None], (lax.axis_size('z'), LANES, p...]
    all_to_all x1, blocking collectives: 27.8 us -> 20.1 us  [shards(): lax.all_to_all(jnp.broadcast_to(summed[None], (peers, HALF, LANES)), ('z'...]
    all_to_all x1, waiting for transfers between devices: 13.2 us -> 8.99 us  [shards(): owned = lax.all_to_all(pair, ('x', 'y'), 0, 0, tiled=True)]
    all_to_all x1, starting transfers between devices: 6.01 us -> 10 us  [shards(): lax.all_to_all(jnp.broadcast_to(flat[None], (lax.axis_size('z'), LANES, p...]
    ppermute x1, waiting for transfers between devices: 0.01 us -> 1.51 us  [shards(): far = lax.ppermute(near, 'core', swap)]
  transfers between devices with their start and end apart: 4 -> 4, of which waited for: 2 -> 3; matrix products, arithmetic and copies ran while one was open for 1% -> 1% of each run, Pallas kernels for 7% -> 14%
where the time goes in v3:
time: 78.5 us; the launch traced here: 77.7 us
  starting transfers between devices  25.5 us (32%)
  blocking collectives  20.1 us (26%)
  Pallas kernels  12.3 us (16%)
  waiting for transfers between devices  11.9 us (15%)
  local copies, waits for them, and re-layouts  5.53 us (7%)
  other arithmetic  1.68 us (2%)
    all_to_all x1, blocking collectives, shards(): lax.all_to_all(jnp.broadcast_to(summed[None], (peers, HALF, LANES)), ('z'...  20.1 us
    all_to_all x1, starting transfers between devices, shards(): lax.all_to_all(jnp.broadcast_to(flat[None], (lax.axis_size('z'), LANES, p...  10 us
    all_to_all x1, starting transfers between devices, shards(): owned = lax.all_to_all(pair, ('x', 'y'), 0, 0, tiled=True)  9.61 us
    all_to_all x1, waiting for transfers between devices, shards(): owned = lax.all_to_all(pair, ('x', 'y'), 0, 0, tiled=True)  8.99 us
    unnamed x16, local copies, waits for them, and re-layouts  4.67 us
    pallas_call x1, Pallas kernels, shards(): pl.pallas_call(send_kernel, out_shape=(moment_shape, jax.ShapeDtypeStruct...  4.66 us
    pallas_call x1, Pallas kernels, shards(): pl.pallas_call(keep_kernel, out_shape=moment_shape, in_specs=[SMEM] + [VM...  3.45 us
    ppermute x1, starting transfers between devices, shards(): far = lax.ppermute(near, 'core', swap)  2.96 us
  transfers between devices with their start and end apart: 4, of which 3 were waited for; matrix products, arithmetic and copies ran while one was open for 1% of the time, Pallas kernels for 14%

profile of v3, /device:TPU:9, one launch (start us, length us, event | category | flops | bytes accessed | tf_op | source)
XLA Modules:
  0.0 77.7 jit_solution(1220650870987971442)
XLA Ops:
  0.6 0.8 bitcast_convert_fusion
  1.4 0.8 %broadcast_in_dim.4 = f32[8,128,128]{2,1,0:T(8,128)} broadcast(f32[128,128]{1,0:T(8,128)S(1)} %bitcast_convert_fusion), dimensions={1,2} | broadcast | bytes 589824 | tf_op jit(solution)/shard_map/broadcast_in_dim | solution.py:223
  2.2 10.0 %all-to-all-start = ((f32[8,128,128]{2,1,0:T(8,128)}), f32[8,128,128]{2,1,0:T(8,128)S(1)}, u32[]{:S(2)}, u32[]{:S(2)}) async-start(f32[8,128,128]{2,1,0:T(8,128)} %broadcast_in_dim.4), calls=%async_computation | async-start | bytes 1048576 | tf_op jit(solution)/shard_map/all_to_all | solution.py:222
  12.3 0.0 copy-start
  12.3 0.8 copy-done
  13.0 0.0 copy-start.2
  13.0 1.0 %copy-done.2 = bf16[64,4096]{1,0:T(8,128)(2,1)S(1)} copy-done((bf16[64,4096]{1,0:T(8,128)(2,1)S(1)}, bf16[64,4096]{1,0:T(8,128)(2,1)}, u32[]{:S(2)}) %copy-start.2) | copy-done | bytes 524312
  14.1 0.0 copy-start.3
  14.1 0.7 copy-done.3
  14.8 0.0 copy-start.4
  14.8 0.7 copy-done.4
  15.5 0.0 copy-start.5
  15.5 0.7 copy-done.5
  16.2 0.0 copy-start.6
  16.2 0.7 copy-done.6
  16.9 0.0 copy-start.7
  16.9 4.7 %values_and_sent_half.1 = (f32[32,32,128]{2,1,0:T(8,128)S(1)}, bf16[256,4096]{1,0:T(8,128)(2,1)S(1)}) custom-call(s32[1]{0:T(128)} %bitcast.2.core_ref, bf16[2,64,128]{2,1,0:T(8,128)(2,1)S(1)} %bitcast.11, f32[2,16,128]{2,1,0:T(8,128)S(1)} %bitcast.14, bf16[64,4096]{1,0:T(8,128)(2,1)S(1)} %copy-done.2, f32[1,4096]{1,0:T(1,128)S(1)} %bitcast.15, ...), custom_call_target="tpu_custom_call" | custom-call | flops 2936012800 | bytes 4194304 | tf_op jit(solution)/shard_map/values_and_sent_half/pallas_call | solution.py:228
  21.6 2.9 %collective-permute-start.1 = (f32[32,32,128]{2,1,0:T(8,128)S(1)}, f32[32,32,128]{2,1,0:T(8,128)S(1)}, u32[]{:S(2)}, u32[]{:S(2)}) collective-permute-start(f32[32,32,128]{2,1,0:T(8,128)S(1)} %get-tuple-element.12), channel_id=1, source_target_pairs={{0,32},{32,0},{1,33},{33,1},{2,34},{34,2},{3,35},{35,3},{4,36},{36... | collective-permute-start | bytes 1572872 | tf_op jit(solution)/shard_map/ppermute | solution.py:240
  24.5 0.0 copy-done.7
  24.5 3.5 %kept_half.1 = f32[32,32,128]{2,1,0:T(8,128)S(1)} custom-call(s32[1]{0:T(128)} %bitcast.2.core_ref, bf16[2,64,128]{2,1,0:T(8,128)(2,1)S(1)} %bitcast.12, bf16[256,4096]{1,0:T(8,128)(2,1)S(1)} %get-tuple-element.11.value_ref, s32[1,4096]{1,0:T(1,128)S(1)} %bitcast.18), custom_call_target="tpu_custom_call" | custom-call | flops 2147483648 | bytes 3145728 | tf_op jit(solution)/shard_map/kept_half/pallas_call | solution.py:241
  28.0 0.0 collective-permute-done.1
  28.0 0.9 %add.3 = f32[32,32,128]{2,1,0:T(8,128)} add(f32[32,32,128]{2,1,0:T(8,128)S(1)} %kept_half.1, f32[32,32,128]{2,1,0:T(8,128)S(1)} %collective-permute-done.1) | non-fusion elementwise | flops 131072 | bytes 1572864 | tf_op jit(solution)/shard_map/add | solution.py:253
  28.8 1.4 %all-to-all-done.near_ref = f32[8,128,128]{2,1,0:T(8,128)S(1)} async-done(((f32[8,128,128]{2,1,0:T(8,128)}), f32[8,128,128]{2,1,0:T(8,128)S(1)}, u32[]{:S(2)}, u32[]{:S(2)}) %all-to-all-start) | async-done | bytes 524320 | tf_op jit(solution)/shard_map/all_to_all | solution.py:222
  30.2 9.6 %all-to-all-start.1 = ((f32[32,32,128]{2,1,0:T(8,128)}), f32[32,32,128]{2,1,0:T(8,128)S(1)}, u32[]{:S(2)}, u32[]{:S(2)}) async-start(f32[32,32,128]{2,1,0:T(8,128)} %add.3), calls=%async_computation.1 | async-start | bytes 1048576 | tf_op jit(solution)/shard_map/all_to_all | solution.py:254
  39.8 0.0 copy-start.1
  39.9 3.0 %collective-permute-start = (f32[8,128,128]{2,1,0:T(8,128)S(1)}, f32[8,128,128]{2,1,0:T(8,128)S(1)}, u32[]{:S(2)}, u32[]{:S(2)}) collective-permute-start(f32[8,128,128]{2,1,0:T(8,128)S(1)} %all-to-all-done.near_ref), channel_id=1, source_target_pairs={{0,32},{32,0},{1,33},{33,1},{2,34},{34,2},{3,35},{35,3},{4,36},{36... | collective-permute-start | bytes 1572872 | tf_op jit(solution)/shard_map/ppermute | solution.py:256
  42.8 1.5 %collective-permute-done.far_ref = f32[8,128,128]{2,1,0:T(8,128)S(1)} collective-permute-done((f32[8,128,128]{2,1,0:T(8,128)S(1)}, f32[8,128,128]{2,1,0:T(8,128)S(1)}, u32[]{:S(2)}, u32[]{:S(2)}) %collective-permute-start) | collective-permute-done | bytes 524320 | tf_op jit(solution)/shard_map/ppermute | solution.py:256
  44.3 2.7 %gram_inverse.1 = (f32[128,128]{1,0:T(8,128)S(1)}, bf16[128,2048]{1,0:T(8,128)(2,1)S(1)}) custom-call(f32[8,128,128]{2,1,0:T(8,128)S(1)} %all-to-all-done.near_ref, f32[8,128,128]{2,1,0:T(8,128)S(1)} %collective-permute-done.far_ref), custom_call_target="tpu_custom_call" | custom-call | flops 4294967296 | bytes 2097152 | tf_op jit(solution)/shard_map/gram_inverse/pallas_call | solution.py:257
  47.0 9.0 %all-to-all-done.1 = f32[32,32,128]{2,1,0:T(8,128)S(1)} async-done(((f32[32,32,128]{2,1,0:T(8,128)}), f32[32,32,128]{2,1,0:T(8,128)S(1)}, u32[]{:S(2)}, u32[]{:S(2)}) %all-to-all-start.1) | async-done | bytes 524320 | tf_op jit(solution)/shard_map/all_to_all | solution.py:254
  56.1 20.1 %all_to_all.15.parts_ref = f32[16,32,128]{2,1,0:T(8,128)S(1)} all-to-all(f32[16,32,128]{2,1,0:T(8,128)S(1)} %broadcast_in_dim.5), channel_id=1, replica_groups=mesh['z'=8,'core'=2,'x'=4,'y'=8] {'z','core'}, dimensions={0} | all-to-all | bytes 524288 | tf_op jit(solution)/shard_map/all_to_all | solution.py:275
  76.1 0.0 copy-done.1
  76.1 1.6 %exposure.1 = (f32[2,64,128]{2,1,0:T(8,128)}, f32[2,64]{1,0:T(2,128)}) custom-call(f32[16,32,128]{2,1,0:T(8,128)S(1)} %all_to_all.15.parts_ref, f32[128,128]{1,0:T(8,128)S(1)} %get-tuple-element.14.inverse_ref, bf16[2,64,128]{2,1,0:T(8,128)(2,1)S(1)} %bitcast.13, bf16[128,2048]{1,0:T(8,128)(2,1)S(1)} %get-tuple-element.15.wide_ref), custom_call_target="tpu_custom_call" | custom-call | tf_op jit(solution)/shard_map/exposure/pallas_call | solution.py:278
  (2 shorter events, 0.1 us)
Async XLA Ops:
  2.2 28.0 %all-to-all-start = ((f32[8,128,128]{2,1,0:T(8,128)}), f32[8,128,128]{2,1,0:T(8,128)S(1)}, u32[]{:S(2)}, u32[]{:S(2)}) async-start(f32[8,128,128]{2,1,0:T(8,128)} %broadcast_in_dim.4), calls=%async_computation | async-start | bytes 1048576 | tf_op jit(solution)/shard_map/all_to_all | solution.py:222
  12.3 0.8 copy-start
  13.0 1.0 %copy-start.2 = (bf16[64,4096]{1,0:T(8,128)(2,1)S(1)}, bf16[64,4096]{1,0:T(8,128)(2,1)}, u32[]{:S(2)}) copy-start(bf16[64,4096]{1,0:T(8,128)(2,1)} %coef_ref.1) | copy-start | bytes 1572868
  14.1 0.7 copy-start.3
  14.8 0.7 copy-start.4
  15.5 0.7 copy-start.5
  16.2 0.7 copy-start.6
  16.9 7.5 %copy-start.7 = (s32[4096]{0:T(1024)S(1)}, s32[4096]{0:T(1024)}, u32[]{:S(2)}) copy-start(s32[4096]{0:T(1024)} %param.10) | copy-start | bytes 49156
  21.6 6.3 %collective-permute-start.1 = (f32[32,32,128]{2,1,0:T(8,128)S(1)}, f32[32,32,128]{2,1,0:T(8,128)S(1)}, u32[]{:S(2)}, u32[]{:S(2)}) collective-permute-start(f32[32,32,128]{2,1,0:T(8,128)S(1)} %get-tuple-element.12), channel_id=1, source_target_pairs={{0,32},{32,0},{1,33},{33,1},{2,34},{34,2},{3,35},{35,3},{4,36},{36... | collective-permute-start | bytes 1572872 | tf_op jit(solution)/shard_map/ppermute | solution.py:240
  30.2 25.8 %all-to-all-start.1 = ((f32[32,32,128]{2,1,0:T(8,128)}), f32[32,32,128]{2,1,0:T(8,128)S(1)}, u32[]{:S(2)}, u32[]{:S(2)}) async-start(f32[32,32,128]{2,1,0:T(8,128)} %add.3), calls=%async_computation.1 | async-start | bytes 1048576 | tf_op jit(solution)/shard_map/all_to_all | solution.py:254
  39.8 36.3 %copy-start.1 = (bf16[2,128,64]{1,2,0:T(8,128)(2,1)S(1)}, bf16[2,128,64]{1,2,0:T(8,128)(2,1)}, u32[]{:S(2)}) copy-start(bf16[2,128,64]{1,2,0:T(8,128)(2,1)} %param.6) | copy-start | bytes 98308
  39.9 4.5 %collective-permute-start = (f32[8,128,128]{2,1,0:T(8,128)S(1)}, f32[8,128,128]{2,1,0:T(8,128)S(1)}, u32[]{:S(2)}, u32[]{:S(2)}) collective-permute-start(f32[8,128,128]{2,1,0:T(8,128)S(1)} %all-to-all-done.near_ref), channel_id=1, source_target_pairs={{0,32},{32,0},{1,33},{33,1},{2,34},{34,2},{3,35},{35,3},{4,36},{36... | collective-permute-start | bytes 1572872 | tf_op jit(solution)/shard_map/ppermute | solution.py:256

commit v4 on v3

--- a/solution.py
+++ b/solution.py
@@ -19,6 +19,7 @@
 LANES = DATES * K
 TILE = 1024
 VMEM = pl.BlockSpec(memory_space=pltpu.VMEM)
+ANY = pl.BlockSpec(memory_space=pl.ANY)
 SMEM = pl.BlockSpec(memory_space=pltpu.SMEM)
 
 
@@ -52,7 +53,7 @@
     )
 
 
-def half_moments(half, wide, value_ref, group_ref, out_ref, total_ref):
+def net_half(half, value_ref, group_ref, total_ref):
     rows = OWNERS * HALF
     trades = value_ref.shape[1]
     for i in range(trades // TILE):
@@ -67,8 +68,11 @@
             total_ref[...] = part
         else:
             total_ref[...] += part
+
+
+def half_moments(wide, total_ref, store):
     step = 256
-    for i in range(rows // step):
+    for i in range(OWNERS * HALF // step):
         span = pl.ds(i * step, step)
         high, middle, low = split(total_ref[span, :])
         moments = (
@@ -76,9 +80,22 @@
             + jnp.dot(middle, wide, preferred_element_type=F32)
             + jnp.dot(low, wide, preferred_element_type=F32)
         )
-        out_ref[pl.ds(i * step // HALF, step // HALF)] = moments.reshape(
-            step // HALF, HALF, LANES
-        )
+        store(i * step // HALF, moments.reshape(step // HALF, HALF, LANES))
+
+
+def payload_kernel(basis_ref, out_ref, narrow_ref, wide_ref, in_sem, out_sems):
+    load = pltpu.make_async_copy(basis_ref, narrow_ref, in_sem)
+    load.start()
+    load.wait()
+    wide_ref[...] = narrow_ref[...].reshape(wide_ref.shape).astype(F32)
+    copies = [
+        pltpu.make_async_copy(wide_ref, out_ref.at[i], out_sems.at[i])
+        for i in range(out_ref.shape[0])
+    ]
+    for copy in copies:
+        copy.start()
+    for copy in copies:
+        copy.wait()
 
 
 def by_path(basis_ref):
@@ -86,28 +103,74 @@
 
 
 def send_kernel(
-    core_ref, basis_ref, fx_ref, coef_ref, floor_ref, group_ref, currency_ref,
-    out_ref, value_ref, total_ref,
+    core_ref, basis_hbm, fx_hbm, coef_hbm, floor_hbm, group_hbm, currency_hbm,
+    out_ref, value_ref,
+    basis_ref, fx_ref, coef_ref, floor_ref, group_ref, currency_ref, total_ref, sems,
 ):
     trades = coef_ref.shape[1]
+    spans = [pl.ds(i * TILE, TILE) for i in range(trades // TILE)]
+    pairs = [
+        (basis_hbm, basis_ref), (fx_hbm, fx_ref), (currency_hbm, currency_ref),
+        (floor_hbm, floor_ref), (group_hbm, group_ref),
+    ]
+    pairs[1:1] = [(coef_hbm.at[:, span], coef_ref.at[:, span]) for span in spans]
+    copies = [
+        pltpu.make_async_copy(source, target, sems.at[i])
+        for i, (source, target) in enumerate(pairs)
+    ]
+    for copy in copies:
+        copy.start()
+    tiles = len(spans)
+    copies[0].wait()
     parts = by_path(basis_ref)
     basis = jnp.concatenate(parts, axis=0)
+    for copy in copies[tiles + 1 : tiles + 4]:
+        copy.wait()
     fx = jnp.concatenate([fx_ref[d].T for d in range(DATES)], axis=0)
     rates = jnp.concatenate(split(fx), axis=1)
-    for i in range(trades // TILE):
-        span = pl.ds(i * TILE, TILE)
+    for i, span in enumerate(spans):
+        copies[1 + i].wait()
         fitted = jnp.dot(basis, coef_ref[:, span], preferred_element_type=F32)
         names = lax.broadcasted_iota(jnp.int32, (3 * NF, TILE), 0) % NF
         chosen = jnp.where(names == currency_ref[:, span], 1.0, 0.0).astype(BF16)
         rate = jnp.dot(rates, chosen, preferred_element_type=F32)
         value_ref[:, span] = (rate * jnp.maximum(fitted, floor_ref[:, span])).astype(BF16)
+    copies[tiles + 4].wait()
+
+    def store(at, moments):
+        out_ref[pl.ds(at, moments.shape[0])] = moments
+
     wide = block_diagonal(*parts)
-    half_moments(1 - core_ref[0], wide, value_ref, group_ref, out_ref, total_ref)
-
-
-def keep_kernel(core_ref, basis_ref, value_ref, group_ref, out_ref, total_ref):
-    wide = block_diagonal(*by_path(basis_ref))
-    half_moments(core_ref[0], wide, value_ref, group_ref, out_ref, total_ref)
+    net_half(1 - core_ref[0], value_ref, group_ref, total_ref)
+    half_moments(wide, total_ref, store)
+
+
+def keep_kernel(core_ref, value_ref, group_hbm, total_ref, group_ref, sem):
+    load = pltpu.make_async_copy(group_hbm, group_ref, sem)
+    load.start()
+    load.wait()
+    net_half(core_ref[0], value_ref, group_ref, total_ref)
+
+
+def pair_kernel(
+    basis_hbm, total_ref, received_ref, out_hbm, basis_ref, sum_ref, in_sem, out_sems
+):
+    load = pltpu.make_async_copy(basis_hbm, basis_ref, in_sem)
+    load.start()
+    load.wait()
+    copies = []
+
+    def store(at, moments):
+        span = pl.ds(at, moments.shape[0])
+        sum_ref[span] = moments + received_ref[span]
+        copies.append(
+            pltpu.make_async_copy(sum_ref.at[span], out_hbm.at[span], out_sems.at[len(copies)])
+        )
+        copies[-1].start()
+
+    half_moments(block_diagonal(*by_path(basis_ref)), total_ref, store)
+    for copy in copies:
+        copy.wait()
 
 
 def eliminate(blocks):
@@ -217,20 +280,42 @@
     names = currency.reshape(1, trades)
     basis = jnp.swapaxes(basis, 1, 2)
     fx_rates = jnp.swapaxes(fx_rates, 1, 2)
-    flat = basis.reshape(LANES, paths).astype(F32)
-
-    near = lax.all_to_all(
-        jnp.broadcast_to(flat[None], (lax.axis_size("z"), LANES, paths)), "z", 0, 0, tiled=True
-    )
+    payload = pl.pallas_call(
+        payload_kernel,
+        out_shape=jax.ShapeDtypeStruct((lax.axis_size("z"), LANES, paths), F32),
+        in_specs=[ANY],
+        out_specs=ANY,
+        scratch_shapes=[
+            pltpu.VMEM((DATES, K, paths), BF16),
+            pltpu.VMEM((LANES, paths), F32),
+            pltpu.SemaphoreType.DMA(()),
+            pltpu.SemaphoreType.DMA((lax.axis_size("z"),)),
+        ],
+        compiler_params=params(),
+        name="basis_payload",
+    )(basis)
+    near = lax.all_to_all(payload, "z", 0, 0, tiled=True)
 
     moment_shape = jax.ShapeDtypeStruct((OWNERS, HALF, LANES), F32)
+    basis_scratch = pltpu.VMEM((DATES, K, paths), BF16)
+    row_scratch = pltpu.VMEM((1, trades), F32)
+    index_scratch = pltpu.VMEM((1, trades), jnp.int32)
     total_scratch = pltpu.VMEM((OWNERS * HALF, DATES * paths), F32)
     send, value = pl.pallas_call(
         send_kernel,
         out_shape=(moment_shape, jax.ShapeDtypeStruct((DATES * paths, trades), BF16)),
-        in_specs=[SMEM] + [VMEM] * 6,
+        in_specs=[SMEM] + [ANY] * 6,
         out_specs=(VMEM, VMEM),
-        scratch_shapes=[total_scratch],
+        scratch_shapes=[
+            basis_scratch,
+            pltpu.VMEM((DATES, NF, paths), F32),
+            pltpu.VMEM((K, trades), BF16),
+            row_scratch,
+            index_scratch,
+            index_scratch,
+            total_scratch,
+            pltpu.SemaphoreType.DMA((5 + trades // TILE,)),
+        ],
         compiler_params=params(),
         cost_estimate=pl.CostEstimate(
             flops=2 * 256 * 4096 * 1400, bytes_accessed=4 * 2**20, transcendentals=0
@@ -238,19 +323,32 @@
         name="values_and_sent_half",
     )(core, basis, fx_rates, coefficients, floor, group, names)
     received = lax.ppermute(send, "core", swap)
-    kept = pl.pallas_call(
+    total = pl.pallas_call(
         keep_kernel,
-        out_shape=moment_shape,
-        in_specs=[SMEM] + [VMEM] * 3,
+        out_shape=jax.ShapeDtypeStruct((OWNERS * HALF, DATES * paths), F32),
+        in_specs=[SMEM, VMEM, ANY],
         out_specs=VMEM,
-        scratch_shapes=[total_scratch],
+        scratch_shapes=[index_scratch, pltpu.SemaphoreType.DMA(())],
         compiler_params=params(),
         cost_estimate=pl.CostEstimate(
             flops=2 * 256 * 4096 * 1024, bytes_accessed=3 * 2**20, transcendentals=0
         ),
         name="kept_half",
-    )(core, basis, value, group)
-    pair = kept + received
+    )(core, value, group)
+    pair = pl.pallas_call(
+        pair_kernel,
+        out_shape=moment_shape,
+        in_specs=[ANY, VMEM, VMEM],
+        out_specs=ANY,
+        scratch_shapes=[
+            basis_scratch,
+            pltpu.VMEM((OWNERS, HALF, LANES), F32),
+            pltpu.SemaphoreType.DMA(()),
+            pltpu.SemaphoreType.DMA((4,)),
+        ],
+        compiler_params=params(),
+        name="pair_moments",
+    )(basis, total, received)
     owned = lax.all_to_all(pair, ("x", "y"), 0, 0, tiled=True)
 
     far = lax.ppermute(near, "core", swap)

time: 78.5 us -> 79.2 us (level)
  Pallas kernels: 12.3 us -> 14.7 us
  other arithmetic: 1.68 us -> 0.05 us
    pallas_call x1 -> x3, Pallas kernels: 3.45 us -> 4.81 us  [the longest x1 2.39 us: shards(): pl.pallas_call(keep_kernel, out_shape=jax.ShapeDtypeStruct((OWNERS * HALF...]
    pallas_call x1, Pallas kernels: 4.66 us -> 5.67 us  [shards(): pl.pallas_call(send_kernel, out_shape=(moment_shape, jax.ShapeDtypeStruct...]
    add x1 -> x0, other arithmetic: 0.87 us -> none  [shards(): pair = kept + received]
    broadcast_in_dim x1 -> x0, local copies, waits for them, and re-layouts: 0.84 us -> none  [shards(): jnp.broadcast_to(flat[None], (lax.axis_size('z'), LANES, paths))]
    unnamed x16 -> x18, local copies, waits for them, and re-layouts: 4.67 us -> 5.43 us
  transfers between devices with their start and end apart: 4 -> 4, of which waited for: 3 -> 3; matrix products, arithmetic and copies ran while one was open for 1% -> 0% of each run, Pallas kernels for 14% -> 16%
where the time goes in v4:
time: 79.2 us; the launch traced here: 78.4 us
  starting transfers between devices  25.5 us (32%)
  blocking collectives  20.7 us (26%)
  Pallas kernels  14.7 us (19%)
  waiting for transfers between devices  11.3 us (14%)
  local copies, waits for them, and re-layouts  5.45 us (7%)
    all_to_all x1, blocking collectives, shards(): lax.all_to_all(jnp.broadcast_to(summed[None], (peers, HALF, LANES)), ('z'...  20.7 us
    all_to_all x1, starting transfers between devices, shards(): near = lax.all_to_all(payload, 'z', 0, 0, tiled=True)  10 us
    all_to_all x1, starting transfers between devices, shards(): owned = lax.all_to_all(pair, ('x', 'y'), 0, 0, tiled=True)  9.61 us
    all_to_all x1, waiting for transfers between devices, shards(): owned = lax.all_to_all(pair, ('x', 'y'), 0, 0, tiled=True)  8.99 us
    pallas_call x1, Pallas kernels, shards(): pl.pallas_call(send_kernel, out_shape=(moment_shape, jax.ShapeDtypeStruct...  5.67 us
    unnamed x18, local copies, waits for them, and re-layouts  5.43 us
    ppermute x1, starting transfers between devices, shards(): far = lax.ppermute(near, 'core', swap)  2.96 us
    ppermute x1, starting transfers between devices, shards(): received = lax.ppermute(send, 'core', swap)  2.87 us
  transfers between devices with their start and end apart: 4, of which 3 were waited for; matrix products, arithmetic and copies ran while one was open for 0% of the time, Pallas kernels for 16%

profile of v4, /device:TPU:9, one launch (start us, length us, event | category | flops | bytes accessed | tf_op | source)
XLA Modules:
  0.0 78.4 jit_solution(12304922610178238408)
XLA Ops:
  0.6 0.0 copy-start
  0.6 0.7 copy-done
  1.4 0.9 %basis_payload.1 = f32[8,128,128]{2,1,0:T(8,128)} custom-call(bf16[2,64,128]{2,1,0:T(8,128)(2,1)S(1)} %bitcast.7), custom_call_target="tpu_custom_call" | custom-call | tf_op jit(solution)/shard_map/basis_payload/pallas_call | solution.py:283
  2.3 10.0 %all-to-all-start = ((f32[8,128,128]{2,1,0:T(8,128)}), f32[8,128,128]{2,1,0:T(8,128)S(1)}, u32[]{:S(2)}, u32[]{:S(2)}) async-start(f32[8,128,128]{2,1,0:T(8,128)} %basis_payload.1), calls=%async_computation | async-start | bytes 1048576 | tf_op jit(solution)/shard_map/all_to_all | solution.py:297
  12.3 0.0 copy-start.1
  12.3 0.8 copy-done.1
  13.1 0.0 copy-start.3
  13.1 1.0 %copy-done.3 = bf16[64,4096]{1,0:T(8,128)(2,1)S(1)} copy-done((bf16[64,4096]{1,0:T(8,128)(2,1)S(1)}, bf16[64,4096]{1,0:T(8,128)(2,1)}, u32[]{:S(2)}) %copy-start.3) | copy-done | bytes 524312
  14.1 0.0 copy-start.4
  14.1 0.7 copy-done.4
  14.9 0.0 copy-start.5
  14.9 0.7 copy-done.5
  15.6 0.0 copy-start.6
  15.6 0.7 copy-done.6
  16.3 0.0 copy-start.7
  16.3 0.7 copy-done.7
  17.0 0.0 copy-start.8
  17.0 5.7 %values_and_sent_half.1 = (f32[32,32,128]{2,1,0:T(8,128)S(1)}, bf16[256,4096]{1,0:T(8,128)(2,1)S(1)}) custom-call(s32[1]{0:T(128)} %bitcast.1.core_ref, bf16[2,64,128]{2,1,0:T(8,128)(2,1)S(1)} %bitcast.8, f32[2,16,128]{2,1,0:T(8,128)S(1)} %bitcast.11, bf16[64,4096]{1,0:T(8,128)(2,1)S(1)} %copy-done.3, f32[1,4096]{1,0:T(1,128)S(1)} %bitcast.12, ...), custom_call_target="tpu_custom_call" | custom-call | flops 2936012800 | bytes 4194304 | tf_op jit(solution)/shard_map/values_and_sent_half/pallas_call | solution.py:304
  22.7 2.9 %collective-permute-start.1 = (f32[32,32,128]{2,1,0:T(8,128)S(1)}, f32[32,32,128]{2,1,0:T(8,128)S(1)}, u32[]{:S(2)}, u32[]{:S(2)}) collective-permute-start(f32[32,32,128]{2,1,0:T(8,128)S(1)} %get-tuple-element.12), channel_id=1, source_target_pairs={{0,32},{32,0},{1,33},{33,1},{2,34},{34,2},{3,35},{35,3},{4,36},{36... | collective-permute-start | bytes 1572872 | tf_op jit(solution)/shard_map/ppermute | solution.py:325
  25.6 0.0 copy-done.8
  25.6 0.0 copy-start.2
  25.6 2.4 %kept_half.1.total_ref = f32[1024,256]{1,0:T(8,128)S(1)} custom-call(s32[1]{0:T(128)} %bitcast.1.core_ref, bf16[256,4096]{1,0:T(8,128)(2,1)S(1)} %get-tuple-element.11.value_ref, s32[1,4096]{1,0:T(1,128)S(1)} %bitcast.15), custom_call_target="tpu_custom_call" | custom-call | flops 2147483648 | bytes 3145728 | tf_op jit(solution)/shard_map/kept_half/pallas_call | solution.py:326
  28.0 0.0 collective-permute-done.1.received_ref
  28.0 0.0 copy-done.2
  28.0 1.5 %pair_moments.1 = f32[32,32,128]{2,1,0:T(8,128)} custom-call(bf16[2,64,128]{2,1,0:T(8,128)(2,1)S(1)} %bitcast.9, f32[1024,256]{1,0:T(8,128)S(1)} %kept_half.1.total_ref, f32[32,32,128]{2,1,0:T(8,128)S(1)} %collective-permute-done.1.received_ref), custom_call_target="tpu_custom_call" | custom-call | tf_op jit(solution)/shard_map/pair_moments/pallas_call | solution.py:338
  29.5 0.8 all-to-all-done.near_ref
  30.3 9.6 %all-to-all-start.1 = ((f32[32,32,128]{2,1,0:T(8,128)}), f32[32,32,128]{2,1,0:T(8,128)S(1)}, u32[]{:S(2)}, u32[]{:S(2)}) async-start(f32[32,32,128]{2,1,0:T(8,128)} %pair_moments.1), calls=%async_computation.1 | async-start | bytes 1048576 | tf_op jit(solution)/shard_map/all_to_all | solution.py:352
  39.9 3.0 %collective-permute-start = (f32[8,128,128]{2,1,0:T(8,128)S(1)}, f32[8,128,128]{2,1,0:T(8,128)S(1)}, u32[]{:S(2)}, u32[]{:S(2)}) collective-permute-start(f32[8,128,128]{2,1,0:T(8,128)S(1)} %all-to-all-done.near_ref), channel_id=1, source_target_pairs={{0,32},{32,0},{1,33},{33,1},{2,34},{34,2},{3,35},{35,3},{4,36},{36... | collective-permute-start | bytes 1572872 | tf_op jit(solution)/shard_map/ppermute | solution.py:354
  42.9 1.5 %collective-permute-done.far_ref = f32[8,128,128]{2,1,0:T(8,128)S(1)} collective-permute-done((f32[8,128,128]{2,1,0:T(8,128)S(1)}, f32[8,128,128]{2,1,0:T(8,128)S(1)}, u32[]{:S(2)}, u32[]{:S(2)}) %collective-permute-start) | collective-permute-done | bytes 524320 | tf_op jit(solution)/shard_map/ppermute | solution.py:354
  44.4 2.7 %gram_inverse.1 = (f32[128,128]{1,0:T(8,128)S(1)}, bf16[128,2048]{1,0:T(8,128)(2,1)S(1)}) custom-call(f32[8,128,128]{2,1,0:T(8,128)S(1)} %all-to-all-done.near_ref, f32[8,128,128]{2,1,0:T(8,128)S(1)} %collective-permute-done.far_ref), custom_call_target="tpu_custom_call" | custom-call | flops 4294967296 | bytes 2097152 | tf_op jit(solution)/shard_map/gram_inverse/pallas_call | solution.py:355
  47.1 9.0 %all-to-all-done.1 = f32[32,32,128]{2,1,0:T(8,128)S(1)} async-done(((f32[32,32,128]{2,1,0:T(8,128)}), f32[32,32,128]{2,1,0:T(8,128)S(1)}, u32[]{:S(2)}, u32[]{:S(2)}) %all-to-all-start.1) | async-done | bytes 524320 | tf_op jit(solution)/shard_map/all_to_all | solution.py:352
  56.1 20.7 %all_to_all.15.parts_ref = f32[16,32,128]{2,1,0:T(8,128)S(1)} all-to-all(f32[16,32,128]{2,1,0:T(8,128)S(1)} %broadcast_in_dim.2), channel_id=1, replica_groups=mesh['z'=8,'core'=2,'x'=4,'y'=8] {'z','core'}, dimensions={0} | all-to-all | bytes 524288 | tf_op jit(solution)/shard_map/all_to_all | solution.py:373
  76.9 1.6 %exposure.1 = (f32[2,64,128]{2,1,0:T(8,128)}, f32[2,64]{1,0:T(2,128)}) custom-call(f32[16,32,128]{2,1,0:T(8,128)S(1)} %all_to_all.15.parts_ref, f32[128,128]{1,0:T(8,128)S(1)} %get-tuple-element.14.inverse_ref, bf16[2,64,128]{2,1,0:T(8,128)(2,1)S(1)} %bitcast.10, bf16[128,2048]{1,0:T(8,128)(2,1)S(1)} %get-tuple-element.15.wide_ref), custom_call_target="tpu_custom_call" | custom-call | tf_op jit(solution)/shard_map/exposure/pallas_call | solution.py:376
  (2 shorter events, 0.1 us)
Async XLA Ops:
  0.6 0.8 copy-start
  2.3 28.0 %all-to-all-start = ((f32[8,128,128]{2,1,0:T(8,128)}), f32[8,128,128]{2,1,0:T(8,128)S(1)}, u32[]{:S(2)}, u32[]{:S(2)}) async-start(f32[8,128,128]{2,1,0:T(8,128)} %basis_payload.1), calls=%async_computation | async-start | bytes 1048576 | tf_op jit(solution)/shard_map/all_to_all | solution.py:297
  12.3 0.8 copy-start.1
  13.1 1.0 %copy-start.3 = (bf16[64,4096]{1,0:T(8,128)(2,1)S(1)}, bf16[64,4096]{1,0:T(8,128)(2,1)}, u32[]{:S(2)}) copy-start(bf16[64,4096]{1,0:T(8,128)(2,1)} %coef_hbm.1) | copy-start | bytes 1572868
  14.1 0.7 copy-start.4
  14.9 0.7 copy-start.5
  15.6 0.7 copy-start.6
  16.3 0.7 copy-start.7
  17.0 8.6 %copy-start.8 = (s32[4096]{0:T(1024)S(1)}, s32[4096]{0:T(1024)}, u32[]{:S(2)}) copy-start(s32[4096]{0:T(1024)} %param.10) | copy-start | bytes 49156
  22.7 5.3 %collective-permute-start.1 = (f32[32,32,128]{2,1,0:T(8,128)S(1)}, f32[32,32,128]{2,1,0:T(8,128)S(1)}, u32[]{:S(2)}, u32[]{:S(2)}) collective-permute-start(f32[32,32,128]{2,1,0:T(8,128)S(1)} %get-tuple-element.12), channel_id=1, source_target_pairs={{0,32},{32,0},{1,33},{33,1},{2,34},{34,2},{3,35},{35,3},{4,36},{36... | collective-permute-start | bytes 1572872 | tf_op jit(solution)/shard_map/ppermute | solution.py:325
  25.6 2.4 %copy-start.2 = (bf16[2,128,64]{1,2,0:T(8,128)(2,1)S(1)}, bf16[2,128,64]{1,2,0:T(8,128)(2,1)}, u32[]{:S(2)}) copy-start(bf16[2,128,64]{1,2,0:T(8,128)(2,1)} %param.6) | copy-start | bytes 98308
  30.3 25.8 %all-to-all-start.1 = ((f32[32,32,128]{2,1,0:T(8,128)}), f32[32,32,128]{2,1,0:T(8,128)S(1)}, u32[]{:S(2)}, u32[]{:S(2)}) async-start(f32[32,32,128]{2,1,0:T(8,128)} %pair_moments.1), calls=%async_computation.1 | async-start | bytes 1048576 | tf_op jit(solution)/shard_map/all_to_all | solution.py:352
  39.9 4.5 %collective-permute-start = (f32[8,128,128]{2,1,0:T(8,128)S(1)}, f32[8,128,128]{2,1,0:T(8,128)S(1)}, u32[]{:S(2)}, u32[]{:S(2)}) collective-permute-start(f32[8,128,128]{2,1,0:T(8,128)S(1)} %all-to-all-done.near_ref), channel_id=1, source_target_pairs={{0,32},{32,0},{1,33},{33,1},{2,34},{34,2},{3,35},{35,3},{4,36},{36... | collective-permute-start | bytes 1572872 | tf_op jit(solution)/shard_map/ppermute | solution.py:354

commit v5 on v3

--- a/solution.py
+++ b/solution.py
@@ -19,6 +19,7 @@
 LANES = DATES * K
 TILE = 1024
 VMEM = pl.BlockSpec(memory_space=pltpu.VMEM)
+ANY = pl.BlockSpec(memory_space=pl.ANY)
 SMEM = pl.BlockSpec(memory_space=pltpu.SMEM)
 
 
@@ -52,7 +53,7 @@
     )
 
 
-def half_moments(half, wide, value_ref, group_ref, out_ref, total_ref):
+def net_half(half, value_ref, group_ref, total_ref):
     rows = OWNERS * HALF
     trades = value_ref.shape[1]
     for i in range(trades // TILE):
@@ -67,8 +68,11 @@
             total_ref[...] = part
         else:
             total_ref[...] += part
+
+
+def half_moments(wide, total_ref, store):
     step = 256
-    for i in range(rows // step):
+    for i in range(OWNERS * HALF // step):
         span = pl.ds(i * step, step)
         high, middle, low = split(total_ref[span, :])
         moments = (
@@ -76,13 +80,22 @@
             + jnp.dot(middle, wide, preferred_element_type=F32)
             + jnp.dot(low, wide, preferred_element_type=F32)
         )
-        out_ref[pl.ds(i * step // HALF, step // HALF)] = moments.reshape(
-            step // HALF, HALF, LANES
-        )
-
-
-def by_path(basis_ref):
-    return [basis_ref[d].astype(F32).T.astype(BF16) for d in range(DATES)]
+        store(i * step // HALF, moments.reshape(step // HALF, HALF, LANES))
+
+
+def payload_kernel(basis_ref, out_ref, rows_ref, wide_ref, sems):
+    wide_ref[...] = basis_ref[...].reshape(wide_ref.shape).astype(F32)
+    copies = [
+        pltpu.make_async_copy(wide_ref, out_ref.at[i], sems.at[i])
+        for i in range(out_ref.shape[0])
+    ]
+    for copy in copies:
+        copy.start()
+    paths = wide_ref.shape[1]
+    for d in range(DATES):
+        rows_ref[d * paths : (d + 1) * paths, :] = wide_ref[d * K : (d + 1) * K, :].T.astype(BF16)
+    for copy in copies:
+        copy.wait()
 
 
 def send_kernel(
@@ -90,8 +103,7 @@
     out_ref, value_ref, total_ref,
 ):
     trades = coef_ref.shape[1]
-    parts = by_path(basis_ref)
-    basis = jnp.concatenate(parts, axis=0)
+    basis = basis_ref[...]
     fx = jnp.concatenate([fx_ref[d].T for d in range(DATES)], axis=0)
     rates = jnp.concatenate(split(fx), axis=1)
     for i in range(trades // TILE):
@@ -101,13 +113,37 @@
         chosen = jnp.where(names == currency_ref[:, span], 1.0, 0.0).astype(BF16)
         rate = jnp.dot(rates, chosen, preferred_element_type=F32)
         value_ref[:, span] = (rate * jnp.maximum(fitted, floor_ref[:, span])).astype(BF16)
-    wide = block_diagonal(*parts)
-    half_moments(1 - core_ref[0], wide, value_ref, group_ref, out_ref, total_ref)
-
-
-def keep_kernel(core_ref, basis_ref, value_ref, group_ref, out_ref, total_ref):
-    wide = block_diagonal(*by_path(basis_ref))
-    half_moments(core_ref[0], wide, value_ref, group_ref, out_ref, total_ref)
+
+    def store(at, moments):
+        out_ref[pl.ds(at, moments.shape[0])] = moments
+
+    net_half(1 - core_ref[0], value_ref, group_ref, total_ref)
+    half_moments(by_date(basis), total_ref, store)
+
+
+def keep_kernel(core_ref, value_ref, group_ref, total_ref):
+    net_half(core_ref[0], value_ref, group_ref, total_ref)
+
+
+def pair_kernel(basis_ref, total_ref, received_ref, out_hbm, sum_ref, sems):
+    copies = []
+
+    def store(at, moments):
+        span = pl.ds(at, moments.shape[0])
+        sum_ref[span] = moments + received_ref[span]
+        copies.append(
+            pltpu.make_async_copy(sum_ref.at[span], out_hbm.at[span], sems.at[len(copies)])
+        )
+        copies[-1].start()
+
+    half_moments(by_date(basis_ref[...]), total_ref, store)
+    for copy in copies:
+        copy.wait()
+
+
+def by_date(basis):
+    paths = basis.shape[0] // DATES
+    return block_diagonal(basis[:paths], basis[paths:])
 
 
 def eliminate(blocks):
@@ -217,40 +253,62 @@
     names = currency.reshape(1, trades)
     basis = jnp.swapaxes(basis, 1, 2)
     fx_rates = jnp.swapaxes(fx_rates, 1, 2)
-    flat = basis.reshape(LANES, paths).astype(F32)
-
-    near = lax.all_to_all(
-        jnp.broadcast_to(flat[None], (lax.axis_size("z"), LANES, paths)), "z", 0, 0, tiled=True
-    )
+    payload, rows = pl.pallas_call(
+        payload_kernel,
+        out_shape=(
+            jax.ShapeDtypeStruct((lax.axis_size("z"), LANES, paths), F32),
+            jax.ShapeDtypeStruct((DATES * paths, K), BF16),
+        ),
+        in_specs=[VMEM],
+        out_specs=(ANY, VMEM),
+        scratch_shapes=[
+            pltpu.VMEM((LANES, paths), F32),
+            pltpu.SemaphoreType.DMA((lax.axis_size("z"),)),
+        ],
+        compiler_params=params(),
+        cost_estimate=pl.CostEstimate(flops=2**31, bytes_accessed=2**24, transcendentals=0),
+        name="basis_payload",
+    )(basis)
+    near = lax.all_to_all(payload, "z", 0, 0, tiled=True)
 
     moment_shape = jax.ShapeDtypeStruct((OWNERS, HALF, LANES), F32)
-    total_scratch = pltpu.VMEM((OWNERS * HALF, DATES * paths), F32)
+    total_shape = (OWNERS * HALF, DATES * paths)
     send, value = pl.pallas_call(
         send_kernel,
         out_shape=(moment_shape, jax.ShapeDtypeStruct((DATES * paths, trades), BF16)),
         in_specs=[SMEM] + [VMEM] * 6,
         out_specs=(VMEM, VMEM),
-        scratch_shapes=[total_scratch],
+        scratch_shapes=[pltpu.VMEM(total_shape, F32)],
         compiler_params=params(),
         cost_estimate=pl.CostEstimate(
             flops=2 * 256 * 4096 * 1400, bytes_accessed=4 * 2**20, transcendentals=0
         ),
         name="values_and_sent_half",
-    )(core, basis, fx_rates, coefficients, floor, group, names)
+    )(core, rows, fx_rates, coefficients, floor, group, names)
     received = lax.ppermute(send, "core", swap)
-    kept = pl.pallas_call(
+    total = pl.pallas_call(
         keep_kernel,
-        out_shape=moment_shape,
-        in_specs=[SMEM] + [VMEM] * 3,
+        out_shape=jax.ShapeDtypeStruct(total_shape, F32),
+        in_specs=[SMEM, VMEM, VMEM],
         out_specs=VMEM,
-        scratch_shapes=[total_scratch],
         compiler_params=params(),
         cost_estimate=pl.CostEstimate(
             flops=2 * 256 * 4096 * 1024, bytes_accessed=3 * 2**20, transcendentals=0
         ),
         name="kept_half",
-    )(core, basis, value, group)
-    pair = kept + received
+    )(core, value, group)
+    pair = pl.pallas_call(
+        pair_kernel,
+        out_shape=moment_shape,
+        in_specs=[VMEM] * 3,
+        out_specs=ANY,
+        scratch_shapes=[
+            pltpu.VMEM((OWNERS, HALF, LANES), F32),
+            pltpu.SemaphoreType.DMA((4,)),
+        ],
+        compiler_params=params(),
+        name="pair_moments",
+    )(rows, total, received)
     owned = lax.all_to_all(pair, ("x", "y"), 0, 0, tiled=True)
 
     far = lax.ppermute(near, "core", swap)

time: 78.5 us -> 75.2 us (0.958)
  waiting for transfers between devices: 11.9 us -> 17.2 us
  local copies, waits for them, and re-layouts: 5.53 us -> 0.8 us
  blocking collectives: 20.1 us -> 17 us
  other arithmetic: 1.68 us -> 0.05 us
  Pallas kernels: 12.3 us -> 13.4 us
    all_to_all x1, waiting for transfers between devices: 1.39 us -> 6.7 us  [shards(): near = lax.all_to_all(payload, 'z', 0, 0, tiled=True)]
    unnamed x16 -> x14, local copies, waits for them, and re-layouts: 4.67 us -> 0.78 us
    all_to_all x1, blocking collectives: 20.1 us -> 17 us  [shards(): lax.all_to_all(jnp.broadcast_to(summed[None], (peers, HALF, LANES)), ('z'...]
    pallas_call x1 -> x3, Pallas kernels: 3.45 us -> 4.57 us  [the longest x1 2.36 us: shards(): pl.pallas_call(keep_kernel, out_shape=jax.ShapeDtypeStruct(total_shape, F...]
    add x1 -> x0, other arithmetic: 0.87 us -> none  [shards(): pair = kept + received]
    broadcast_in_dim x1 -> x0, local copies, waits for them, and re-layouts: 0.84 us -> none  [shards(): jnp.broadcast_to(flat[None], (lax.axis_size('z'), LANES, paths))]
  transfers between devices with their start and end apart: 4 -> 4, of which waited for: 3 -> 3; matrix products, arithmetic and copies ran while one was open for 1% -> 0% of each run, Pallas kernels for 14% -> 15%
where the time goes in v5:
time: 75.2 us; the launch traced here: 74.7 us
  starting transfers between devices  25.5 us (34%)
  waiting for transfers between devices  17.2 us (23%)
  blocking collectives  17 us (23%)
  Pallas kernels  13.4 us (18%)
  local copies, waits for them, and re-layouts  0.8 us (1%)
  between operations  0.78 us (1%)
    all_to_all x1, blocking collectives, shards(): lax.all_to_all(jnp.broadcast_to(summed[None], (peers, HALF, LANES)), ('z'...  17 us
    all_to_all x1, starting transfers between devices, shards(): near = lax.all_to_all(payload, 'z', 0, 0, tiled=True)  10 us
    all_to_all x1, starting transfers between devices, shards(): owned = lax.all_to_all(pair, ('x', 'y'), 0, 0, tiled=True)  9.6 us
    all_to_all x1, waiting for transfers between devices, shards(): owned = lax.all_to_all(pair, ('x', 'y'), 0, 0, tiled=True)  8.98 us
    all_to_all x1, waiting for transfers between devices, shards(): near = lax.all_to_all(payload, 'z', 0, 0, tiled=True)  6.7 us
    pallas_call x1, Pallas kernels, shards(): pl.pallas_call(send_kernel, out_shape=(moment_shape, jax.ShapeDtypeStruct...  4.6 us
    ppermute x1, starting transfers between devices, shards(): far = lax.ppermute(near, 'core', swap)  2.96 us
    ppermute x1, starting transfers between devices, shards(): received = lax.ppermute(send, 'core', swap)  2.87 us
  transfers between devices with their start and end apart: 4, of which 3 were waited for; matrix products, arithmetic and copies ran while one was open for 0% of the time, Pallas kernels for 15%

profile of v5, /device:TPU:9, one launch (start us, length us, event | category | flops | bytes accessed | tf_op | source)
XLA Modules:
  0.0 74.7 jit_solution(5839001285471556163)
XLA Ops:
  0.6 0.0 copy-start
  0.6 0.7 %copy-done = bf16[2,128,64]{1,2,0:T(8,128)(2,1)S(1)} copy-done((bf16[2,128,64]{1,2,0:T(8,128)(2,1)S(1)}, bf16[2,128,64]{1,2,0:T(8,128)(2,1)}, u32[]{:S(2)}) %copy-start) | copy-done | bytes 32792
  1.4 0.0 copy-start.2
  1.4 0.0 copy-start.3
  1.4 0.0 copy-start.4
  1.4 0.0 copy-start.5
  1.4 0.0 copy-start.6
  1.4 0.9 %basis_payload.1 = (f32[8,128,128]{2,1,0:T(8,128)}, bf16[256,64]{1,0:T(8,128)(2,1)S(1)}) custom-call(bf16[2,64,128]{2,1,0:T(8,128)(2,1)S(1)} %bitcast.7), custom_call_target="tpu_custom_call" | custom-call | flops 2147483648 | bytes 16777216 | tf_op jit(solution)/shard_map/basis_payload/pallas_call | solution.py:256
  2.3 10.0 %all-to-all-start = ((f32[8,128,128]{2,1,0:T(8,128)}), f32[8,128,128]{2,1,0:T(8,128)S(1)}, u32[]{:S(2)}, u32[]{:S(2)}) async-start(f32[8,128,128]{2,1,0:T(8,128)} %get-tuple-element.12), calls=%async_computation | async-start | bytes 1048576 | tf_op jit(solution)/shard_map/all_to_all | solution.py:272
  12.3 0.0 copy-done.2
  12.3 0.0 copy-done.3
  12.4 0.0 copy-done.4
  12.4 0.0 copy-done.5
  12.4 0.0 copy-done.6
  12.4 4.6 %values_and_sent_half.1 = (f32[32,32,128]{2,1,0:T(8,128)S(1)}, bf16[256,4096]{1,0:T(8,128)(2,1)S(1)}) custom-call(s32[1]{0:T(128)} %bitcast.1.core_ref, bf16[256,64]{1,0:T(8,128)(2,1)S(1)} %get-tuple-element.14.basis_ref, f32[2,16,128]{2,1,0:T(8,128)S(1)} %bitcast.9, bf16[64,4096]{1,0:T(8,128)(2,1)S(1)} %copy-done.2, f32[1,4096]{1,0:T(1,128)S(1)} %bitcast.10, ...), custom_call_target="tpu_custom_call" | custom-call | flops 2936012800 | bytes 4194304 | tf_op jit(solution)/shard_map/values_and_sent_half/pallas_call | solution.py:276
  17.0 2.9 %collective-permute-start.1 = (f32[32,32,128]{2,1,0:T(8,128)S(1)}, f32[32,32,128]{2,1,0:T(8,128)S(1)}, u32[]{:S(2)}, u32[]{:S(2)}) collective-permute-start(f32[32,32,128]{2,1,0:T(8,128)S(1)} %get-tuple-element.16), channel_id=1, source_target_pairs={{0,32},{32,0},{1,33},{33,1},{2,34},{34,2},{3,35},{35,3},{4,36},{36... | collective-permute-start | bytes 1572872 | tf_op jit(solution)/shard_map/ppermute | solution.py:288
  19.9 2.4 %kept_half.1.total_ref = f32[1024,256]{1,0:T(8,128)S(1)} custom-call(s32[1]{0:T(128)} %bitcast.1.core_ref, bf16[256,4096]{1,0:T(8,128)(2,1)S(1)} %get-tuple-element.15.value_ref, s32[1,4096]{1,0:T(1,128)S(1)} %bitcast.13), custom_call_target="tpu_custom_call" | custom-call | flops 2147483648 | bytes 3145728 | tf_op jit(solution)/shard_map/kept_half/pallas_call | solution.py:289
  22.2 0.0 collective-permute-done.1.received_ref
  22.2 1.3 %pair_moments.1 = f32[32,32,128]{2,1,0:T(8,128)} custom-call(bf16[256,64]{1,0:T(8,128)(2,1)S(1)} %get-tuple-element.14.basis_ref, f32[1024,256]{1,0:T(8,128)S(1)} %kept_half.1.total_ref, f32[32,32,128]{2,1,0:T(8,128)S(1)} %collective-permute-done.1.received_ref), custom_call_target="tpu_custom_call" | custom-call | tf_op jit(solution)/shard_map/pair_moments/pallas_call | solution.py:300
  23.6 6.7 %all-to-all-done.near_ref = f32[8,128,128]{2,1,0:T(8,128)S(1)} async-done(((f32[8,128,128]{2,1,0:T(8,128)}), f32[8,128,128]{2,1,0:T(8,128)S(1)}, u32[]{:S(2)}, u32[]{:S(2)}) %all-to-all-start) | async-done | bytes 524320 | tf_op jit(solution)/shard_map/all_to_all | solution.py:272
  30.3 9.6 %all-to-all-start.1 = ((f32[32,32,128]{2,1,0:T(8,128)}), f32[32,32,128]{2,1,0:T(8,128)S(1)}, u32[]{:S(2)}, u32[]{:S(2)}) async-start(f32[32,32,128]{2,1,0:T(8,128)} %pair_moments.1), calls=%async_computation.1 | async-start | bytes 1048576 | tf_op jit(solution)/shard_map/all_to_all | solution.py:312
  39.9 0.0 copy-start.1
  39.9 3.0 %collective-permute-start = (f32[8,128,128]{2,1,0:T(8,128)S(1)}, f32[8,128,128]{2,1,0:T(8,128)S(1)}, u32[]{:S(2)}, u32[]{:S(2)}) collective-permute-start(f32[8,128,128]{2,1,0:T(8,128)S(1)} %all-to-all-done.near_ref), channel_id=1, source_target_pairs={{0,32},{32,0},{1,33},{33,1},{2,34},{34,2},{3,35},{35,3},{4,36},{36... | collective-permute-start | bytes 1572872 | tf_op jit(solution)/shard_map/ppermute | solution.py:314
  42.9 1.5 %collective-permute-done.far_ref = f32[8,128,128]{2,1,0:T(8,128)S(1)} collective-permute-done((f32[8,128,128]{2,1,0:T(8,128)S(1)}, f32[8,128,128]{2,1,0:T(8,128)S(1)}, u32[]{:S(2)}, u32[]{:S(2)}) %collective-permute-start) | collective-permute-done | bytes 524320 | tf_op jit(solution)/shard_map/ppermute | solution.py:314
  44.4 2.7 %gram_inverse.1 = (f32[128,128]{1,0:T(8,128)S(1)}, bf16[128,2048]{1,0:T(8,128)(2,1)S(1)}) custom-call(f32[8,128,128]{2,1,0:T(8,128)S(1)} %all-to-all-done.near_ref, f32[8,128,128]{2,1,0:T(8,128)S(1)} %collective-permute-done.far_ref), custom_call_target="tpu_custom_call" | custom-call | flops 4294967296 | bytes 2097152 | tf_op jit(solution)/shard_map/gram_inverse/pallas_call | solution.py:315
  47.1 9.0 %all-to-all-done.1 = f32[32,32,128]{2,1,0:T(8,128)S(1)} async-done(((f32[32,32,128]{2,1,0:T(8,128)}), f32[32,32,128]{2,1,0:T(8,128)S(1)}, u32[]{:S(2)}, u32[]{:S(2)}) %all-to-all-start.1) | async-done | bytes 524320 | tf_op jit(solution)/shard_map/all_to_all | solution.py:312
  56.1 17.0 %all_to_all.15.parts_ref = f32[16,32,128]{2,1,0:T(8,128)S(1)} all-to-all(f32[16,32,128]{2,1,0:T(8,128)S(1)} %broadcast_in_dim.2), channel_id=1, replica_groups=mesh['z'=8,'core'=2,'x'=4,'y'=8] {'z','core'}, dimensions={0} | all-to-all | bytes 524288 | tf_op jit(solution)/shard_map/all_to_all | solution.py:333
  73.1 0.0 copy-done.1
  73.1 1.5 %exposure.1 = (f32[2,64,128]{2,1,0:T(8,128)}, f32[2,64]{1,0:T(2,128)}) custom-call(f32[16,32,128]{2,1,0:T(8,128)S(1)} %all_to_all.15.parts_ref, f32[128,128]{1,0:T(8,128)S(1)} %get-tuple-element.18.inverse_ref, bf16[2,64,128]{2,1,0:T(8,128)(2,1)S(1)} %bitcast.8, bf16[128,2048]{1,0:T(8,128)(2,1)S(1)} %get-tuple-element.19.wide_ref), custom_call_target="tpu_custom_call" | custom-call | tf_op jit(solution)/shard_map/exposure/pallas_call | solution.py:336
  (2 shorter events, 0.1 us)
Async XLA Ops:
  0.6 0.8 %copy-start = (bf16[2,128,64]{1,2,0:T(8,128)(2,1)S(1)}, bf16[2,128,64]{1,2,0:T(8,128)(2,1)}, u32[]{:S(2)}) copy-start(bf16[2,128,64]{1,2,0:T(8,128)(2,1)} %param.6) | copy-start | bytes 98308
  1.4 10.9 %copy-start.2 = (bf16[64,4096]{1,0:T(8,128)(2,1)S(1)}, bf16[64,4096]{1,0:T(8,128)(2,1)}, u32[]{:S(2)}) copy-start(bf16[64,4096]{1,0:T(8,128)(2,1)} %coef_ref.1) | copy-start | bytes 1572868
  1.4 11.0 %copy-start.3 = (f32[2,128,16]{1,2,0:T(8,128)S(1)}, f32[2,128,16]{1,2,0:T(8,128)}, u32[]{:S(2)}) copy-start(f32[2,128,16]{1,2,0:T(8,128)} %param.7) | copy-start | bytes 49156
  1.4 11.0 %copy-start.4 = (f32[4096]{0:T(1024)S(1)}, f32[4096]{0:T(1024)}, u32[]{:S(2)}) copy-start(f32[4096]{0:T(1024)} %param.9) | copy-start | bytes 49156
  1.4 11.0 %copy-start.5 = (s32[4096]{0:T(1024)S(1)}, s32[4096]{0:T(1024)}, u32[]{:S(2)}) copy-start(s32[4096]{0:T(1024)} %param.11) | copy-start | bytes 49156
  1.4 11.0 %copy-start.6 = (s32[4096]{0:T(1024)S(1)}, s32[4096]{0:T(1024)}, u32[]{:S(2)}) copy-start(s32[4096]{0:T(1024)} %param.10) | copy-start | bytes 49156
  2.3 28.0 %all-to-all-start = ((f32[8,128,128]{2,1,0:T(8,128)}), f32[8,128,128]{2,1,0:T(8,128)S(1)}, u32[]{:S(2)}, u32[]{:S(2)}) async-start(f32[8,128,128]{2,1,0:T(8,128)} %get-tuple-element.12), calls=%async_computation | async-start | bytes 1048576 | tf_op jit(solution)/shard_map/all_to_all | solution.py:272
  17.0 5.3 %collective-permute-start.1 = (f32[32,32,128]{2,1,0:T(8,128)S(1)}, f32[32,32,128]{2,1,0:T(8,128)S(1)}, u32[]{:S(2)}, u32[]{:S(2)}) collective-permute-start(f32[32,32,128]{2,1,0:T(8,128)S(1)} %get-tuple-element.16), channel_id=1, source_target_pairs={{0,32},{32,0},{1,33},{33,1},{2,34},{34,2},{3,35},{35,3},{4,36},{36... | collective-permute-start | bytes 1572872 | tf_op jit(solution)/shard_map/ppermute | solution.py:288
  30.3 25.8 %all-to-all-start.1 = ((f32[32,32,128]{2,1,0:T(8,128)}), f32[32,32,128]{2,1,0:T(8,128)S(1)}, u32[]{:S(2)}, u32[]{:S(2)}) async-start(f32[32,32,128]{2,1,0:T(8,128)} %pair_moments.1), calls=%async_computation.1 | async-start | bytes 1048576 | tf_op jit(solution)/shard_map/all_to_all | solution.py:312
  39.9 33.2 %copy-start.1 = (bf16[2,128,64]{1,2,0:T(8,128)(2,1)S(1)}, bf16[2,128,64]{1,2,0:T(8,128)(2,1)}, u32[]{:S(2)}) copy-start(bf16[2,128,64]{1,2,0:T(8,128)(2,1)} %param.6) | copy-start | bytes 98308
  39.9 4.5 %collective-permute-start = (f32[8,128,128]{2,1,0:T(8,128)S(1)}, f32[8,128,128]{2,1,0:T(8,128)S(1)}, u32[]{:S(2)}, u32[]{:S(2)}) collective-permute-start(f32[8,128,128]{2,1,0:T(8,128)S(1)} %all-to-all-done.near_ref), channel_id=1, source_target_pairs={{0,32},{32,0},{1,33},{33,1},{2,34},{34,2},{3,35},{35,3},{4,36},{36... | collective-permute-start | bytes 1572872 | tf_op jit(solution)/shard_map/ppermute | solution.py:314

commit v6 on v5

--- a/solution.py
+++ b/solution.py
@@ -202,16 +202,9 @@
 
 
 def exposure_kernel(
-    parts_ref, inverse_ref, basis_ref, wide_ref, exposure_ref, expected_ref
+    halves_ref, inverse_ref, basis_ref, wide_ref, exposure_ref, expected_ref
 ):
-    peers = parts_ref.shape[0]
-    halves = []
-    for h in range(2):
-        total = parts_ref[h]
-        for i in range(h + 2, peers, 2):
-            total = total + parts_ref[i]
-        halves.append(total)
-    moments = jnp.concatenate(halves, axis=0)
+    moments = halves_ref[...].reshape(SET_DEV, LANES)
     beta = jnp.dot(moments, inverse_ref[...], precision=HIGHEST, preferred_element_type=F32)
     lane = lax.broadcasted_iota(jnp.int32, (SET_DEV, LANES), 1)
     rows = jnp.concatenate(
@@ -329,10 +322,10 @@
 
     summed = jnp.sum(owned, axis=0)
     inverse, summed = lax.optimization_barrier((inverse, summed))
-    peers = lax.axis_size("z") * lax.axis_size("core")
     parts = lax.all_to_all(
-        jnp.broadcast_to(summed[None], (peers, HALF, LANES)), ("z", "core"), 0, 0, tiled=True
-    )
+        jnp.broadcast_to(summed[None], (lax.axis_size("z"), HALF, LANES)), "z", 0, 0, tiled=True
+    )
+    halves = lax.all_gather(jnp.sum(parts, axis=0), "core")
     exposure, expected = pl.pallas_call(
         exposure_kernel,
         out_shape=(
@@ -343,7 +336,7 @@
         out_specs=(VMEM, VMEM),
         compiler_params=params(),
         name="exposure",
-    )(parts, inverse, basis, wide)
+    )(halves, inverse, basis, wide)
     return jnp.swapaxes(exposure, 1, 2), expected
 
 

time: 75.2 us -> 73.8 us (0.981)
  blocking collectives: 17 us -> 15.7 us
    all_to_all x1, blocking collectives: 17 us -> 10.3 us  [shards(): lax.all_to_all(jnp.broadcast_to(summed[None], (lax.axis_size('z'), HALF,...]
    all_gather x0 -> x1, blocking collectives: none -> 5.37 us  [shards(): halves = lax.all_gather(jnp.sum(parts, axis=0), 'core')]
where the time goes in v6:
time: 73.8 us; the launch traced here: 73.4 us
  starting transfers between devices  25.5 us (35%)
  waiting for transfers between devices  17.2 us (23%)
  blocking collectives  15.7 us (21%)
  Pallas kernels  13.4 us (18%)
  local copies, waits for them, and re-layouts  0.79 us (1%)
  between operations  0.78 us (1%)
    all_to_all x1, blocking collectives, shards(): lax.all_to_all(jnp.broadcast_to(summed[None], (lax.axis_size('z'), HALF,...  10.3 us
    all_to_all x1, starting transfers between devices, shards(): near = lax.all_to_all(payload, 'z', 0, 0, tiled=True)  10 us
    all_to_all x1, starting transfers between devices, shards(): owned = lax.all_to_all(pair, ('x', 'y'), 0, 0, tiled=True)  9.6 us
    all_to_all x1, waiting for transfers between devices, shards(): owned = lax.all_to_all(pair, ('x', 'y'), 0, 0, tiled=True)  8.98 us
    all_to_all x1, waiting for transfers between devices, shards(): near = lax.all_to_all(payload, 'z', 0, 0, tiled=True)  6.71 us
    all_gather x1, blocking collectives, shards(): halves = lax.all_gather(jnp.sum(parts, axis=0), 'core')  5.37 us
    pallas_call x1, Pallas kernels, shards(): pl.pallas_call(send_kernel, out_shape=(moment_shape, jax.ShapeDtypeStruct...  4.59 us
    ppermute x1, starting transfers between devices, shards(): far = lax.ppermute(near, 'core', swap)  2.96 us
  transfers between devices with their start and end apart: 4, of which 3 were waited for; matrix products, arithmetic and copies ran while one was open for 0% of the time, Pallas kernels for 15%

profile of v6, /device:TPU:9, one launch (start us, length us, event | category | flops | bytes accessed | tf_op | source)
XLA Modules:
  0.0 73.4 jit_solution(11725495660842623025)
XLA Ops:
  0.6 0.0 copy-start
  0.6 0.7 %copy-done = bf16[2,128,64]{1,2,0:T(8,128)(2,1)S(1)} copy-done((bf16[2,128,64]{1,2,0:T(8,128)(2,1)S(1)}, bf16[2,128,64]{1,2,0:T(8,128)(2,1)}, u32[]{:S(2)}) %copy-start) | copy-done | bytes 32792
  1.4 0.0 copy-start.2
  1.4 0.0 copy-start.3
  1.4 0.0 copy-start.4
  1.4 0.0 copy-start.5
  1.4 0.0 copy-start.6
  1.4 0.9 %basis_payload.1 = (f32[8,128,128]{2,1,0:T(8,128)}, bf16[256,64]{1,0:T(8,128)(2,1)S(1)}) custom-call(bf16[2,64,128]{2,1,0:T(8,128)(2,1)S(1)} %bitcast.9), custom_call_target="tpu_custom_call" | custom-call | flops 2147483648 | bytes 16777216 | tf_op jit(solution)/shard_map/basis_payload/pallas_call | solution.py:249
  2.3 10.0 %all-to-all-start = ((f32[8,128,128]{2,1,0:T(8,128)}), f32[8,128,128]{2,1,0:T(8,128)S(1)}, u32[]{:S(2)}, u32[]{:S(2)}) async-start(f32[8,128,128]{2,1,0:T(8,128)} %get-tuple-element.12), calls=%async_computation | async-start | bytes 1048576 | tf_op jit(solution)/shard_map/all_to_all | solution.py:265
  12.3 0.0 copy-done.2
  12.3 0.0 copy-done.3
  12.4 0.0 copy-done.4
  12.4 0.0 copy-done.5
  12.4 0.0 copy-done.6
  12.4 4.6 %values_and_sent_half.1 = (f32[32,32,128]{2,1,0:T(8,128)S(1)}, bf16[256,4096]{1,0:T(8,128)(2,1)S(1)}) custom-call(s32[1]{0:T(128)} %bitcast.1.core_ref, bf16[256,64]{1,0:T(8,128)(2,1)S(1)} %get-tuple-element.14.basis_ref, f32[2,16,128]{2,1,0:T(8,128)S(1)} %bitcast.11, bf16[64,4096]{1,0:T(8,128)(2,1)S(1)} %copy-done.2, f32[1,4096]{1,0:T(1,128)S(1)} %bitcast.12, ...), custom_call_target="tpu_custom_call" | custom-call | flops 2936012800 | bytes 4194304 | tf_op jit(solution)/shard_map/values_and_sent_half/pallas_call | solution.py:269
  17.0 2.9 %collective-permute-start.1 = (f32[32,32,128]{2,1,0:T(8,128)S(1)}, f32[32,32,128]{2,1,0:T(8,128)S(1)}, u32[]{:S(2)}, u32[]{:S(2)}) collective-permute-start(f32[32,32,128]{2,1,0:T(8,128)S(1)} %get-tuple-element.16), channel_id=1, source_target_pairs={{0,32},{32,0},{1,33},{33,1},{2,34},{34,2},{3,35},{35,3},{4,36},{36... | collective-permute-start | bytes 1572872 | tf_op jit(solution)/shard_map/ppermute | solution.py:281
  19.9 2.4 %kept_half.1.total_ref = f32[1024,256]{1,0:T(8,128)S(1)} custom-call(s32[1]{0:T(128)} %bitcast.1.core_ref, bf16[256,4096]{1,0:T(8,128)(2,1)S(1)} %get-tuple-element.15.value_ref, s32[1,4096]{1,0:T(1,128)S(1)} %bitcast.15), custom_call_target="tpu_custom_call" | custom-call | flops 2147483648 | bytes 3145728 | tf_op jit(solution)/shard_map/kept_half/pallas_call | solution.py:282
  22.2 0.0 collective-permute-done.1.received_ref
  22.2 1.3 %pair_moments.1 = f32[32,32,128]{2,1,0:T(8,128)} custom-call(bf16[256,64]{1,0:T(8,128)(2,1)S(1)} %get-tuple-element.14.basis_ref, f32[1024,256]{1,0:T(8,128)S(1)} %kept_half.1.total_ref, f32[32,32,128]{2,1,0:T(8,128)S(1)} %collective-permute-done.1.received_ref), custom_call_target="tpu_custom_call" | custom-call | tf_op jit(solution)/shard_map/pair_moments/pallas_call | solution.py:293
  23.6 6.7 %all-to-all-done.near_ref = f32[8,128,128]{2,1,0:T(8,128)S(1)} async-done(((f32[8,128,128]{2,1,0:T(8,128)}), f32[8,128,128]{2,1,0:T(8,128)S(1)}, u32[]{:S(2)}, u32[]{:S(2)}) %all-to-all-start) | async-done | bytes 524320 | tf_op jit(solution)/shard_map/all_to_all | solution.py:265
  30.3 9.6 %all-to-all-start.1 = ((f32[32,32,128]{2,1,0:T(8,128)}), f32[32,32,128]{2,1,0:T(8,128)S(1)}, u32[]{:S(2)}, u32[]{:S(2)}) async-start(f32[32,32,128]{2,1,0:T(8,128)} %pair_moments.1), calls=%async_computation.1 | async-start | bytes 1048576 | tf_op jit(solution)/shard_map/all_to_all | solution.py:305
  39.9 0.0 copy-start.1
  39.9 3.0 %collective-permute-start = (f32[8,128,128]{2,1,0:T(8,128)S(1)}, f32[8,128,128]{2,1,0:T(8,128)S(1)}, u32[]{:S(2)}, u32[]{:S(2)}) collective-permute-start(f32[8,128,128]{2,1,0:T(8,128)S(1)} %all-to-all-done.near_ref), channel_id=1, source_target_pairs={{0,32},{32,0},{1,33},{33,1},{2,34},{34,2},{3,35},{35,3},{4,36},{36... | collective-permute-start | bytes 1572872 | tf_op jit(solution)/shard_map/ppermute | solution.py:307
  42.9 1.5 %collective-permute-done.far_ref = f32[8,128,128]{2,1,0:T(8,128)S(1)} collective-permute-done((f32[8,128,128]{2,1,0:T(8,128)S(1)}, f32[8,128,128]{2,1,0:T(8,128)S(1)}, u32[]{:S(2)}, u32[]{:S(2)}) %collective-permute-start) | collective-permute-done | bytes 524320 | tf_op jit(solution)/shard_map/ppermute | solution.py:307
  44.4 2.7 %gram_inverse.1 = (f32[128,128]{1,0:T(8,128)S(1)}, bf16[128,2048]{1,0:T(8,128)(2,1)S(1)}) custom-call(f32[8,128,128]{2,1,0:T(8,128)S(1)} %all-to-all-done.near_ref, f32[8,128,128]{2,1,0:T(8,128)S(1)} %collective-permute-done.far_ref), custom_call_target="tpu_custom_call" | custom-call | flops 4294967296 | bytes 2097152 | tf_op jit(solution)/shard_map/gram_inverse/pallas_call | solution.py:308
  47.1 9.0 %all-to-all-done.1 = f32[32,32,128]{2,1,0:T(8,128)S(1)} async-done(((f32[32,32,128]{2,1,0:T(8,128)}), f32[32,32,128]{2,1,0:T(8,128)S(1)}, u32[]{:S(2)}, u32[]{:S(2)}) %all-to-all-start.1) | async-done | bytes 524320 | tf_op jit(solution)/shard_map/all_to_all | solution.py:305
  56.1 10.3 %all_to_all.15 = f32[8,32,128]{2,1,0:T(8,128)S(1)} all-to-all(f32[8,32,128]{2,1,0:T(8,128)S(1)} %broadcast_in_dim.2), channel_id=1, replica_groups=mesh['z'=8,'core'=2,'x'=4,'y'=8] {'z'}, dimensions={0} | all-to-all | bytes 262144 | tf_op jit(solution)/shard_map/all_to_all | solution.py:325
  66.4 5.4 %all-gather = f32[64,128]{1,0:T(8,128)S(1)} all-gather(f32[32,128]{1,0:T(8,128)S(1)} %reduce_sum.19), channel_id=2, replica_groups=mesh['z'=8,'core'=2,'x'=4,'y'=8] {'core'}, dimensions={0}, use_global_device_ids=true | all-gather | bytes 49152 | tf_op jit(solution)/shard_map/all_gather | solution.py:328
  71.8 0.0 copy-done.1
  71.8 1.5 %exposure.1 = (f32[2,64,128]{2,1,0:T(8,128)}, f32[2,64]{1,0:T(2,128)}) custom-call(f32[2,32,128]{2,1,0:T(8,128)S(1)} %bitcast.8, f32[128,128]{1,0:T(8,128)S(1)} %get-tuple-element.18.inverse_ref, bf16[2,64,128]{2,1,0:T(8,128)(2,1)S(1)} %bitcast.10, bf16[128,2048]{1,0:T(8,128)(2,1)S(1)} %get-tuple-element.19.wide_ref), custom_call_target="tpu_custom_call" | custom-call | tf_op jit(solution)/shard_map/exposure/pallas_call | solution.py:329
  (3 shorter events, 0.1 us)
Async XLA Ops:
  0.6 0.8 %copy-start = (bf16[2,128,64]{1,2,0:T(8,128)(2,1)S(1)}, bf16[2,128,64]{1,2,0:T(8,128)(2,1)}, u32[]{:S(2)}) copy-start(bf16[2,128,64]{1,2,0:T(8,128)(2,1)} %param.6) | copy-start | bytes 98308
  1.4 10.9 %copy-start.2 = (bf16[64,4096]{1,0:T(8,128)(2,1)S(1)}, bf16[64,4096]{1,0:T(8,128)(2,1)}, u32[]{:S(2)}) copy-start(bf16[64,4096]{1,0:T(8,128)(2,1)} %coef_ref.1) | copy-start | bytes 1572868
  1.4 10.9 %copy-start.3 = (f32[2,128,16]{1,2,0:T(8,128)S(1)}, f32[2,128,16]{1,2,0:T(8,128)}, u32[]{:S(2)}) copy-start(f32[2,128,16]{1,2,0:T(8,128)} %param.7) | copy-start | bytes 49156
  1.4 11.0 %copy-start.4 = (f32[4096]{0:T(1024)S(1)}, f32[4096]{0:T(1024)}, u32[]{:S(2)}) copy-start(f32[4096]{0:T(1024)} %param.9) | copy-start | bytes 49156
  1.4 11.0 %copy-start.5 = (s32[4096]{0:T(1024)S(1)}, s32[4096]{0:T(1024)}, u32[]{:S(2)}) copy-start(s32[4096]{0:T(1024)} %param.11) | copy-start | bytes 49156
  1.4 11.0 %copy-start.6 = (s32[4096]{0:T(1024)S(1)}, s32[4096]{0:T(1024)}, u32[]{:S(2)}) copy-start(s32[4096]{0:T(1024)} %param.10) | copy-start | bytes 49156
  2.3 28.0 %all-to-all-start = ((f32[8,128,128]{2,1,0:T(8,128)}), f32[8,128,128]{2,1,0:T(8,128)S(1)}, u32[]{:S(2)}, u32[]{:S(2)}) async-start(f32[8,128,128]{2,1,0:T(8,128)} %get-tuple-element.12), calls=%async_computation | async-start | bytes 1048576 | tf_op jit(solution)/shard_map/all_to_all | solution.py:265
  17.0 5.3 %collective-permute-start.1 = (f32[32,32,128]{2,1,0:T(8,128)S(1)}, f32[32,32,128]{2,1,0:T(8,128)S(1)}, u32[]{:S(2)}, u32[]{:S(2)}) collective-permute-start(f32[32,32,128]{2,1,0:T(8,128)S(1)} %get-tuple-element.16), channel_id=1, source_target_pairs={{0,32},{32,0},{1,33},{33,1},{2,34},{34,2},{3,35},{35,3},{4,36},{36... | collective-permute-start | bytes 1572872 | tf_op jit(solution)/shard_map/ppermute | solution.py:281
  30.3 25.8 %all-to-all-start.1 = ((f32[32,32,128]{2,1,0:T(8,128)}), f32[32,32,128]{2,1,0:T(8,128)S(1)}, u32[]{:S(2)}, u32[]{:S(2)}) async-start(f32[32,32,128]{2,1,0:T(8,128)} %pair_moments.1), calls=%async_computation.1 | async-start | bytes 1048576 | tf_op jit(solution)/shard_map/all_to_all | solution.py:305
  39.9 31.9 %copy-start.1 = (bf16[2,128,64]{1,2,0:T(8,128)(2,1)S(1)}, bf16[2,128,64]{1,2,0:T(8,128)(2,1)}, u32[]{:S(2)}) copy-start(bf16[2,128,64]{1,2,0:T(8,128)(2,1)} %param.6) | copy-start | bytes 98308
  39.9 4.5 %collective-permute-start = (f32[8,128,128]{2,1,0:T(8,128)S(1)}, f32[8,128,128]{2,1,0:T(8,128)S(1)}, u32[]{:S(2)}, u32[]{:S(2)}) collective-permute-start(f32[8,128,128]{2,1,0:T(8,128)S(1)} %all-to-all-done.near_ref), channel_id=1, source_target_pairs={{0,32},{32,0},{1,33},{33,1},{2,34},{34,2},{3,35},{35,3},{4,36},{36... | collective-permute-start | bytes 1572872 | tf_op jit(solution)/shard_map/ppermute | solution.py:307

commit v7 on v6

--- a/solution.py
+++ b/solution.py
@@ -83,19 +83,13 @@
         store(i * step // HALF, moments.reshape(step // HALF, HALF, LANES))
 
 
-def payload_kernel(basis_ref, out_ref, rows_ref, wide_ref, sems):
-    wide_ref[...] = basis_ref[...].reshape(wide_ref.shape).astype(F32)
-    copies = [
-        pltpu.make_async_copy(wide_ref, out_ref.at[i], sems.at[i])
-        for i in range(out_ref.shape[0])
-    ]
-    for copy in copies:
-        copy.start()
-    paths = wide_ref.shape[1]
+def payload_kernel(basis_ref, out_ref, rows_ref):
+    wide = basis_ref[...].reshape(out_ref.shape[1:]).astype(F32)
+    for i in range(out_ref.shape[0]):
+        out_ref[i] = wide
+    paths = wide.shape[1]
     for d in range(DATES):
-        rows_ref[d * paths : (d + 1) * paths, :] = wide_ref[d * K : (d + 1) * K, :].T.astype(BF16)
-    for copy in copies:
-        copy.wait()
+        rows_ref[d * paths : (d + 1) * paths, :] = wide[d * K : (d + 1) * K, :].T.astype(BF16)
 
 
 def send_kernel(
@@ -125,20 +119,12 @@
     net_half(core_ref[0], value_ref, group_ref, total_ref)
 
 
-def pair_kernel(basis_ref, total_ref, received_ref, out_hbm, sum_ref, sems):
-    copies = []
-
+def pair_kernel(basis_ref, total_ref, received_ref, out_ref):
     def store(at, moments):
         span = pl.ds(at, moments.shape[0])
-        sum_ref[span] = moments + received_ref[span]
-        copies.append(
-            pltpu.make_async_copy(sum_ref.at[span], out_hbm.at[span], sems.at[len(copies)])
-        )
-        copies[-1].start()
+        out_ref[span] = moments + received_ref[span]
 
     half_moments(by_date(basis_ref[...]), total_ref, store)
-    for copy in copies:
-        copy.wait()
 
 
 def by_date(basis):
@@ -210,19 +196,19 @@
     rows = jnp.concatenate(
         [jnp.where(lane < K, beta, 0.0), jnp.where(lane < K, 0.0, beta)], axis=0
     )
-    stacked = jnp.concatenate(split(rows), axis=0)
+    high, middle, low = split(rows)
+    upper = jnp.concatenate([high, middle], axis=1)
 
     def exposed(basis):
-        smooth = jnp.dot(stacked, basis, preferred_element_type=F32)
-        return jnp.maximum(
-            smooth[:LANES] + smooth[LANES : 2 * LANES] + smooth[2 * LANES :], 0.0
-        )
+        twice = jnp.concatenate([basis, basis], axis=0)
+        smooth = jnp.dot(upper, twice, preferred_element_type=F32)
+        return jnp.maximum(smooth + jnp.dot(low, basis, preferred_element_type=F32), 0.0)
 
     paths = basis_ref.shape[2]
     exposure = exposed(basis_ref[...].reshape(LANES, paths))
     exposure_ref[...] = exposure.reshape(DATES, SET_DEV, paths)
     total = jnp.zeros((LANES, 128), F32)
-    step = 512
+    step = 256
     for i in range(PATHS // step):
         part = exposed(wide_ref[:, i * step : (i + 1) * step])
         for j in range(step // 128):
@@ -253,11 +239,7 @@
             jax.ShapeDtypeStruct((DATES * paths, K), BF16),
         ),
         in_specs=[VMEM],
-        out_specs=(ANY, VMEM),
-        scratch_shapes=[
-            pltpu.VMEM((LANES, paths), F32),
-            pltpu.SemaphoreType.DMA((lax.axis_size("z"),)),
-        ],
+        out_specs=(VMEM, VMEM),
         compiler_params=params(),
         cost_estimate=pl.CostEstimate(flops=2**31, bytes_accessed=2**24, transcendentals=0),
         name="basis_payload",
@@ -294,11 +276,7 @@
         pair_kernel,
         out_shape=moment_shape,
         in_specs=[VMEM] * 3,
-        out_specs=ANY,
-        scratch_shapes=[
-            pltpu.VMEM((OWNERS, HALF, LANES), F32),
-            pltpu.SemaphoreType.DMA((4,)),
-        ],
+        out_specs=VMEM,
         compiler_params=params(),
         name="pair_moments",
     )(rows, total, received)

time: 73.8 us -> 73.7 us (level)
  no operation moved by 1% of the time
where the time goes in v7:
time: 73.7 us; the launch traced here: 73.2 us
  starting transfers between devices  25.5 us (35%)
  waiting for transfers between devices  17.1 us (23%)
  blocking collectives  15.7 us (21%)
  Pallas kernels  13.3 us (18%)
  local copies, waits for them, and re-layouts  0.79 us (1%)
  between operations  0.76 us (1%)
    all_to_all x1, blocking collectives, shards(): lax.all_to_all(jnp.broadcast_to(summed[None], (lax.axis_size('z'), HALF,...  10.3 us
    all_to_all x1, starting transfers between devices, shards(): near = lax.all_to_all(payload, 'z', 0, 0, tiled=True)  10 us
    all_to_all x1, starting transfers between devices, shards(): owned = lax.all_to_all(pair, ('x', 'y'), 0, 0, tiled=True)  9.6 us
    all_to_all x1, waiting for transfers between devices, shards(): owned = lax.all_to_all(pair, ('x', 'y'), 0, 0, tiled=True)  8.98 us
    all_to_all x1, waiting for transfers between devices, shards(): near = lax.all_to_all(payload, 'z', 0, 0, tiled=True)  6.63 us
    all_gather x1, blocking collectives, shards(): halves = lax.all_gather(jnp.sum(parts, axis=0), 'core')  5.37 us
    pallas_call x1, Pallas kernels, shards(): pl.pallas_call(send_kernel, out_shape=(moment_shape, jax.ShapeDtypeStruct...  4.6 us
    ppermute x1, starting transfers between devices, shards(): far = lax.ppermute(near, 'core', swap)  2.96 us
  transfers between devices with their start and end apart: 4, of which 3 were waited for; matrix products, arithmetic and copies ran while one was open for 0% of the time, Pallas kernels for 15%

profile of v7, /device:TPU:9, one launch (start us, length us, event | category | flops | bytes accessed | tf_op | source)
XLA Modules:
  0.0 73.2 jit_solution(7660185179107612212)
XLA Ops:
  0.6 0.0 copy-start
  0.6 0.7 %copy-done = bf16[2,128,64]{1,2,0:T(8,128)(2,1)S(1)} copy-done((bf16[2,128,64]{1,2,0:T(8,128)(2,1)S(1)}, bf16[2,128,64]{1,2,0:T(8,128)(2,1)}, u32[]{:S(2)}) %copy-start) | copy-done | bytes 32792
  1.4 0.0 copy-start.2
  1.4 0.0 copy-start.3
  1.4 0.0 copy-start.4
  1.4 0.0 copy-start.5
  1.4 0.0 copy-start.6
  1.4 0.8 %basis_payload.1 = (f32[8,128,128]{2,1,0:T(8,128)}, bf16[256,64]{1,0:T(8,128)(2,1)S(1)}) custom-call(bf16[2,64,128]{2,1,0:T(8,128)(2,1)S(1)} %bitcast.9), custom_call_target="tpu_custom_call" | custom-call | flops 2147483648 | bytes 16777216 | tf_op jit(solution)/shard_map/basis_payload/pallas_call | solution.py:235
  2.3 10.0 %all-to-all-start = ((f32[8,128,128]{2,1,0:T(8,128)}), f32[8,128,128]{2,1,0:T(8,128)S(1)}, u32[]{:S(2)}, u32[]{:S(2)}) async-start(f32[8,128,128]{2,1,0:T(8,128)} %get-tuple-element.12), calls=%async_computation | async-start | bytes 1048576 | tf_op jit(solution)/shard_map/all_to_all | solution.py:247
  12.3 0.0 copy-done.2
  12.3 0.0 copy-done.3
  12.3 0.0 copy-done.4
  12.3 0.0 copy-done.5
  12.3 0.0 copy-done.6
  12.3 4.6 %values_and_sent_half.1 = (f32[32,32,128]{2,1,0:T(8,128)S(1)}, bf16[256,4096]{1,0:T(8,128)(2,1)S(1)}) custom-call(s32[1]{0:T(128)} %bitcast.1.core_ref, bf16[256,64]{1,0:T(8,128)(2,1)S(1)} %get-tuple-element.14.basis_ref, f32[2,16,128]{2,1,0:T(8,128)S(1)} %bitcast.11, bf16[64,4096]{1,0:T(8,128)(2,1)S(1)} %copy-done.2, f32[1,4096]{1,0:T(1,128)S(1)} %bitcast.12, ...), custom_call_target="tpu_custom_call" | custom-call | flops 2936012800 | bytes 4194304 | tf_op jit(solution)/shard_map/values_and_sent_half/pallas_call | solution.py:251
  16.9 2.9 %collective-permute-start.1 = (f32[32,32,128]{2,1,0:T(8,128)S(1)}, f32[32,32,128]{2,1,0:T(8,128)S(1)}, u32[]{:S(2)}, u32[]{:S(2)}) collective-permute-start(f32[32,32,128]{2,1,0:T(8,128)S(1)} %get-tuple-element.16), channel_id=1, source_target_pairs={{0,32},{32,0},{1,33},{33,1},{2,34},{34,2},{3,35},{35,3},{4,36},{36... | collective-permute-start | bytes 1572872 | tf_op jit(solution)/shard_map/ppermute | solution.py:263
  19.8 2.4 %kept_half.1.total_ref = f32[1024,256]{1,0:T(8,128)S(1)} custom-call(s32[1]{0:T(128)} %bitcast.1.core_ref, bf16[256,4096]{1,0:T(8,128)(2,1)S(1)} %get-tuple-element.15.value_ref, s32[1,4096]{1,0:T(1,128)S(1)} %bitcast.15), custom_call_target="tpu_custom_call" | custom-call | flops 2147483648 | bytes 3145728 | tf_op jit(solution)/shard_map/kept_half/pallas_call | solution.py:264
  22.2 0.0 collective-permute-done.1.received_ref
  22.2 1.4 %pair_moments.1 = f32[32,32,128]{2,1,0:T(8,128)} custom-call(bf16[256,64]{1,0:T(8,128)(2,1)S(1)} %get-tuple-element.14.basis_ref, f32[1024,256]{1,0:T(8,128)S(1)} %kept_half.1.total_ref, f32[32,32,128]{2,1,0:T(8,128)S(1)} %collective-permute-done.1.received_ref), custom_call_target="tpu_custom_call" | custom-call | tf_op jit(solution)/shard_map/pair_moments/pallas_call | solution.py:275
  23.6 6.6 %all-to-all-done.near_ref = f32[8,128,128]{2,1,0:T(8,128)S(1)} async-done(((f32[8,128,128]{2,1,0:T(8,128)}), f32[8,128,128]{2,1,0:T(8,128)S(1)}, u32[]{:S(2)}, u32[]{:S(2)}) %all-to-all-start) | async-done | bytes 524320 | tf_op jit(solution)/shard_map/all_to_all | solution.py:247
  30.3 9.6 %all-to-all-start.1 = ((f32[32,32,128]{2,1,0:T(8,128)}), f32[32,32,128]{2,1,0:T(8,128)S(1)}, u32[]{:S(2)}, u32[]{:S(2)}) async-start(f32[32,32,128]{2,1,0:T(8,128)} %pair_moments.1), calls=%async_computation.1 | async-start | bytes 1048576 | tf_op jit(solution)/shard_map/all_to_all | solution.py:283
  39.9 0.0 copy-start.1
  39.9 3.0 %collective-permute-start = (f32[8,128,128]{2,1,0:T(8,128)S(1)}, f32[8,128,128]{2,1,0:T(8,128)S(1)}, u32[]{:S(2)}, u32[]{:S(2)}) collective-permute-start(f32[8,128,128]{2,1,0:T(8,128)S(1)} %all-to-all-done.near_ref), channel_id=1, source_target_pairs={{0,32},{32,0},{1,33},{33,1},{2,34},{34,2},{3,35},{35,3},{4,36},{36... | collective-permute-start | bytes 1572872 | tf_op jit(solution)/shard_map/ppermute | solution.py:285
  42.8 1.5 %collective-permute-done.far_ref = f32[8,128,128]{2,1,0:T(8,128)S(1)} collective-permute-done((f32[8,128,128]{2,1,0:T(8,128)S(1)}, f32[8,128,128]{2,1,0:T(8,128)S(1)}, u32[]{:S(2)}, u32[]{:S(2)}) %collective-permute-start) | collective-permute-done | bytes 524320 | tf_op jit(solution)/shard_map/ppermute | solution.py:285
  44.4 2.7 %gram_inverse.1 = (f32[128,128]{1,0:T(8,128)S(1)}, bf16[128,2048]{1,0:T(8,128)(2,1)S(1)}) custom-call(f32[8,128,128]{2,1,0:T(8,128)S(1)} %all-to-all-done.near_ref, f32[8,128,128]{2,1,0:T(8,128)S(1)} %collective-permute-done.far_ref), custom_call_target="tpu_custom_call" | custom-call | flops 4294967296 | bytes 2097152 | tf_op jit(solution)/shard_map/gram_inverse/pallas_call | solution.py:286
  47.0 9.0 %all-to-all-done.1 = f32[32,32,128]{2,1,0:T(8,128)S(1)} async-done(((f32[32,32,128]{2,1,0:T(8,128)}), f32[32,32,128]{2,1,0:T(8,128)S(1)}, u32[]{:S(2)}, u32[]{:S(2)}) %all-to-all-start.1) | async-done | bytes 524320 | tf_op jit(solution)/shard_map/all_to_all | solution.py:283
  56.1 10.3 %all_to_all.15 = f32[8,32,128]{2,1,0:T(8,128)S(1)} all-to-all(f32[8,32,128]{2,1,0:T(8,128)S(1)} %broadcast_in_dim.2), channel_id=1, replica_groups=mesh['z'=8,'core'=2,'x'=4,'y'=8] {'z'}, dimensions={0} | all-to-all | bytes 262144 | tf_op jit(solution)/shard_map/all_to_all | solution.py:303
  66.4 5.4 %all-gather = f32[64,128]{1,0:T(8,128)S(1)} all-gather(f32[32,128]{1,0:T(8,128)S(1)} %reduce_sum.19), channel_id=2, replica_groups=mesh['z'=8,'core'=2,'x'=4,'y'=8] {'core'}, dimensions={0}, use_global_device_ids=true | all-gather | bytes 49152 | tf_op jit(solution)/shard_map/all_gather | solution.py:306
  71.8 0.0 copy-done.1
  71.8 1.4 %exposure.1 = (f32[2,64,128]{2,1,0:T(8,128)}, f32[2,64]{1,0:T(2,128)}) custom-call(f32[2,32,128]{2,1,0:T(8,128)S(1)} %bitcast.8, f32[128,128]{1,0:T(8,128)S(1)} %get-tuple-element.18.inverse_ref, bf16[2,64,128]{2,1,0:T(8,128)(2,1)S(1)} %bitcast.10, bf16[128,2048]{1,0:T(8,128)(2,1)S(1)} %get-tuple-element.19.wide_ref), custom_call_target="tpu_custom_call" | custom-call | tf_op jit(solution)/shard_map/exposure/pallas_call | solution.py:307
  (3 shorter events, 0.1 us)
Async XLA Ops:
  0.6 0.8 %copy-start = (bf16[2,128,64]{1,2,0:T(8,128)(2,1)S(1)}, bf16[2,128,64]{1,2,0:T(8,128)(2,1)}, u32[]{:S(2)}) copy-start(bf16[2,128,64]{1,2,0:T(8,128)(2,1)} %param.6) | copy-start | bytes 98308
  1.4 10.9 %copy-start.2 = (bf16[64,4096]{1,0:T(8,128)(2,1)S(1)}, bf16[64,4096]{1,0:T(8,128)(2,1)}, u32[]{:S(2)}) copy-start(bf16[64,4096]{1,0:T(8,128)(2,1)} %coef_ref.1) | copy-start | bytes 1572868
  1.4 10.9 %copy-start.3 = (f32[2,128,16]{1,2,0:T(8,128)S(1)}, f32[2,128,16]{1,2,0:T(8,128)}, u32[]{:S(2)}) copy-start(f32[2,128,16]{1,2,0:T(8,128)} %param.7) | copy-start | bytes 49156
  1.4 10.9 %copy-start.4 = (f32[4096]{0:T(1024)S(1)}, f32[4096]{0:T(1024)}, u32[]{:S(2)}) copy-start(f32[4096]{0:T(1024)} %param.9) | copy-start | bytes 49156
  1.4 10.9 %copy-start.5 = (s32[4096]{0:T(1024)S(1)}, s32[4096]{0:T(1024)}, u32[]{:S(2)}) copy-start(s32[4096]{0:T(1024)} %param.11) | copy-start | bytes 49156
  1.4 10.9 %copy-start.6 = (s32[4096]{0:T(1024)S(1)}, s32[4096]{0:T(1024)}, u32[]{:S(2)}) copy-start(s32[4096]{0:T(1024)} %param.10) | copy-start | bytes 49156
  2.3 28.0 %all-to-all-start = ((f32[8,128,128]{2,1,0:T(8,128)}), f32[8,128,128]{2,1,0:T(8,128)S(1)}, u32[]{:S(2)}, u32[]{:S(2)}) async-start(f32[8,128,128]{2,1,0:T(8,128)} %get-tuple-element.12), calls=%async_computation | async-start | bytes 1048576 | tf_op jit(solution)/shard_map/all_to_all | solution.py:247
  16.9 5.2 %collective-permute-start.1 = (f32[32,32,128]{2,1,0:T(8,128)S(1)}, f32[32,32,128]{2,1,0:T(8,128)S(1)}, u32[]{:S(2)}, u32[]{:S(2)}) collective-permute-start(f32[32,32,128]{2,1,0:T(8,128)S(1)} %get-tuple-element.16), channel_id=1, source_target_pairs={{0,32},{32,0},{1,33},{33,1},{2,34},{34,2},{3,35},{35,3},{4,36},{36... | collective-permute-start | bytes 1572872 | tf_op jit(solution)/shard_map/ppermute | solution.py:263
  30.3 25.8 %all-to-all-start.1 = ((f32[32,32,128]{2,1,0:T(8,128)}), f32[32,32,128]{2,1,0:T(8,128)S(1)}, u32[]{:S(2)}, u32[]{:S(2)}) async-start(f32[32,32,128]{2,1,0:T(8,128)} %pair_moments.1), calls=%async_computation.1 | async-start | bytes 1048576 | tf_op jit(solution)/shard_map/all_to_all | solution.py:283
  39.9 31.9 %copy-start.1 = (bf16[2,128,64]{1,2,0:T(8,128)(2,1)S(1)}, bf16[2,128,64]{1,2,0:T(8,128)(2,1)}, u32[]{:S(2)}) copy-start(bf16[2,128,64]{1,2,0:T(8,128)(2,1)} %param.6) | copy-start | bytes 98308
  39.9 4.5 %collective-permute-start = (f32[8,128,128]{2,1,0:T(8,128)S(1)}, f32[8,128,128]{2,1,0:T(8,128)S(1)}, u32[]{:S(2)}, u32[]{:S(2)}) collective-permute-start(f32[8,128,128]{2,1,0:T(8,128)S(1)} %all-to-all-done.near_ref), channel_id=1, source_target_pairs={{0,32},{32,0},{1,33},{33,1},{2,34},{34,2},{3,35},{35,3},{4,36},{36... | collective-permute-start | bytes 1572872 | tf_op jit(solution)/shard_map/ppermute | solution.py:285

commit v8 on v7

--- a/solution.py
+++ b/solution.py
@@ -84,7 +84,7 @@
 
 
 def payload_kernel(basis_ref, out_ref, rows_ref):
-    wide = basis_ref[...].reshape(out_ref.shape[1:]).astype(F32)
+    wide = basis_ref[...]
     for i in range(out_ref.shape[0]):
         out_ref[i] = wide
     paths = wide.shape[1]
@@ -238,12 +238,13 @@
             jax.ShapeDtypeStruct((lax.axis_size("z"), LANES, paths), F32),
             jax.ShapeDtypeStruct((DATES * paths, K), BF16),
         ),
-        in_specs=[VMEM],
+        grid=(1,),
+        in_specs=[pl.BlockSpec((LANES, paths), lambda i: (0, 0))],
         out_specs=(VMEM, VMEM),
-        compiler_params=params(),
+        compiler_params=params(allow_input_fusion=[True]),
         cost_estimate=pl.CostEstimate(flops=2**31, bytes_accessed=2**24, transcendentals=0),
         name="basis_payload",
-    )(basis)
+    )(basis.reshape(LANES, paths).astype(F32))
     near = lax.all_to_all(payload, "z", 0, 0, tiled=True)
 
     moment_shape = jax.ShapeDtypeStruct((OWNERS, HALF, LANES), F32)

time: 73.7 us -> 73.7 us (level)
  other arithmetic: 0.06 us -> 0.82 us
  local copies, waits for them, and re-layouts: 0.79 us -> 0.04 us
    convert_element_type x0 -> x1, other arithmetic: none -> 0.77 us  [shards(): basis.reshape(LANES, paths).astype(F32)]
    unnamed x14 -> x12, local copies, waits for them, and re-layouts: 0.78 us -> 0.03 us
where the time goes in v8:
time: 73.7 us; the launch traced here: 73.2 us
  starting transfers between devices  25.5 us (35%)
  waiting for transfers between devices  17.1 us (23%)
  blocking collectives  15.7 us (21%)
  Pallas kernels  13.3 us (18%)
  other arithmetic  0.82 us (1%)
  between operations  0.77 us (1%)
    all_to_all x1, blocking collectives, shards(): lax.all_to_all(jnp.broadcast_to(summed[None], (lax.axis_size('z'), HALF,...  10.3 us
    all_to_all x1, starting transfers between devices, shards(): near = lax.all_to_all(payload, 'z', 0, 0, tiled=True)  10 us
    all_to_all x1, starting transfers between devices, shards(): owned = lax.all_to_all(pair, ('x', 'y'), 0, 0, tiled=True)  9.6 us
    all_to_all x1, waiting for transfers between devices, shards(): owned = lax.all_to_all(pair, ('x', 'y'), 0, 0, tiled=True)  8.99 us
    all_to_all x1, waiting for transfers between devices, shards(): near = lax.all_to_all(payload, 'z', 0, 0, tiled=True)  6.62 us
    all_gather x1, blocking collectives, shards(): halves = lax.all_gather(jnp.sum(parts, axis=0), 'core')  5.37 us
    pallas_call x1, Pallas kernels, shards(): pl.pallas_call(send_kernel, out_shape=(moment_shape, jax.ShapeDtypeStruct...  4.61 us
    ppermute x1, starting transfers between devices, shards(): far = lax.ppermute(near, 'core', swap)  2.96 us
  transfers between devices with their start and end apart: 4, of which 3 were waited for; matrix products, arithmetic and copies ran while one was open for 0% of the time, Pallas kernels for 15%

profile of v8, /device:TPU:9, one launch (start us, length us, event | category | flops | bytes accessed | tf_op | source)
XLA Modules:
  0.0 73.2 jit_solution(11282127642893510068)
XLA Ops:
  0.6 0.8 %bitcast_convert_fusion.basis_ref = f32[128,128]{1,0:T(8,128)S(1)} fusion(bf16[2,128,64]{1,2,0:T(8,128)(2,1)} %param.6), kind=kLoop, calls=%fused_computation | loop fusion | flops 16384 | bytes 98304 | tf_op jit(solution)/shard_map/convert_element_type | solution.py:247
  1.4 0.0 copy-start.1
  1.4 0.0 copy-start.2
  1.4 0.0 copy-start.3
  1.4 0.0 copy-start.4
  1.4 0.0 copy-start.5
  1.4 0.8 %basis_payload.1 = (f32[8,128,128]{2,1,0:T(8,128)}, bf16[256,64]{1,0:T(8,128)(2,1)S(1)}) custom-call(f32[128,128]{1,0:T(8,128)S(1)} %bitcast_convert_fusion.basis_ref), custom_call_target="tpu_custom_call" | custom-call | flops 2147483648 | bytes 16777216 | tf_op jit(solution)/shard_map/basis_payload/pallas_call | solution.py:235
  2.3 10.0 %all-to-all-start = ((f32[8,128,128]{2,1,0:T(8,128)}), f32[8,128,128]{2,1,0:T(8,128)S(1)}, u32[]{:S(2)}, u32[]{:S(2)}) async-start(f32[8,128,128]{2,1,0:T(8,128)} %get-tuple-element.12), calls=%async_computation | async-start | bytes 1048576 | tf_op jit(solution)/shard_map/all_to_all | solution.py:248
  12.3 0.0 copy-done.1
  12.3 0.0 copy-done.2
  12.3 0.0 copy-done.3
  12.3 0.0 copy-done.4
  12.4 0.0 copy-done.5
  12.4 4.6 %values_and_sent_half.1 = (f32[32,32,128]{2,1,0:T(8,128)S(1)}, bf16[256,4096]{1,0:T(8,128)(2,1)S(1)}) custom-call(s32[1]{0:T(128)} %bitcast.2.core_ref, bf16[256,64]{1,0:T(8,128)(2,1)S(1)} %get-tuple-element.14.basis_ref, f32[2,16,128]{2,1,0:T(8,128)S(1)} %bitcast.14, bf16[64,4096]{1,0:T(8,128)(2,1)S(1)} %copy-done.1, f32[1,4096]{1,0:T(1,128)S(1)} %bitcast.15, ...), custom_call_target="tpu_custom_call" | custom-call | flops 2936012800 | bytes 4194304 | tf_op jit(solution)/shard_map/values_and_sent_half/pallas_call | solution.py:252
  17.0 2.8 %collective-permute-start.1 = (f32[32,32,128]{2,1,0:T(8,128)S(1)}, f32[32,32,128]{2,1,0:T(8,128)S(1)}, u32[]{:S(2)}, u32[]{:S(2)}) collective-permute-start(f32[32,32,128]{2,1,0:T(8,128)S(1)} %get-tuple-element.16), channel_id=1, source_target_pairs={{0,32},{32,0},{1,33},{33,1},{2,34},{34,2},{3,35},{35,3},{4,36},{36... | collective-permute-start | bytes 1572872 | tf_op jit(solution)/shard_map/ppermute | solution.py:264
  19.8 2.4 %kept_half.1.total_ref = f32[1024,256]{1,0:T(8,128)S(1)} custom-call(s32[1]{0:T(128)} %bitcast.2.core_ref, bf16[256,4096]{1,0:T(8,128)(2,1)S(1)} %get-tuple-element.15.value_ref, s32[1,4096]{1,0:T(1,128)S(1)} %bitcast.18), custom_call_target="tpu_custom_call" | custom-call | flops 2147483648 | bytes 3145728 | tf_op jit(solution)/shard_map/kept_half/pallas_call | solution.py:265
  22.2 0.0 collective-permute-done.1.received_ref
  22.2 1.4 %pair_moments.1 = f32[32,32,128]{2,1,0:T(8,128)} custom-call(bf16[256,64]{1,0:T(8,128)(2,1)S(1)} %get-tuple-element.14.basis_ref, f32[1024,256]{1,0:T(8,128)S(1)} %kept_half.1.total_ref, f32[32,32,128]{2,1,0:T(8,128)S(1)} %collective-permute-done.1.received_ref), custom_call_target="tpu_custom_call" | custom-call | tf_op jit(solution)/shard_map/pair_moments/pallas_call | solution.py:276
  23.7 6.6 %all-to-all-done.near_ref = f32[8,128,128]{2,1,0:T(8,128)S(1)} async-done(((f32[8,128,128]{2,1,0:T(8,128)}), f32[8,128,128]{2,1,0:T(8,128)S(1)}, u32[]{:S(2)}, u32[]{:S(2)}) %all-to-all-start) | async-done | bytes 524320 | tf_op jit(solution)/shard_map/all_to_all | solution.py:248
  30.3 9.6 %all-to-all-start.1 = ((f32[32,32,128]{2,1,0:T(8,128)}), f32[32,32,128]{2,1,0:T(8,128)S(1)}, u32[]{:S(2)}, u32[]{:S(2)}) async-start(f32[32,32,128]{2,1,0:T(8,128)} %pair_moments.1), calls=%async_computation.1 | async-start | bytes 1048576 | tf_op jit(solution)/shard_map/all_to_all | solution.py:284
  39.9 0.0 copy-start
  39.9 3.0 %collective-permute-start = (f32[8,128,128]{2,1,0:T(8,128)S(1)}, f32[8,128,128]{2,1,0:T(8,128)S(1)}, u32[]{:S(2)}, u32[]{:S(2)}) collective-permute-start(f32[8,128,128]{2,1,0:T(8,128)S(1)} %all-to-all-done.near_ref), channel_id=1, source_target_pairs={{0,32},{32,0},{1,33},{33,1},{2,34},{34,2},{3,35},{35,3},{4,36},{36... | collective-permute-start | bytes 1572872 | tf_op jit(solution)/shard_map/ppermute | solution.py:286
  42.9 1.5 %collective-permute-done.far_ref = f32[8,128,128]{2,1,0:T(8,128)S(1)} collective-permute-done((f32[8,128,128]{2,1,0:T(8,128)S(1)}, f32[8,128,128]{2,1,0:T(8,128)S(1)}, u32[]{:S(2)}, u32[]{:S(2)}) %collective-permute-start) | collective-permute-done | bytes 524320 | tf_op jit(solution)/shard_map/ppermute | solution.py:286
  44.4 2.7 %gram_inverse.1 = (f32[128,128]{1,0:T(8,128)S(1)}, bf16[128,2048]{1,0:T(8,128)(2,1)S(1)}) custom-call(f32[8,128,128]{2,1,0:T(8,128)S(1)} %all-to-all-done.near_ref, f32[8,128,128]{2,1,0:T(8,128)S(1)} %collective-permute-done.far_ref), custom_call_target="tpu_custom_call" | custom-call | flops 4294967296 | bytes 2097152 | tf_op jit(solution)/shard_map/gram_inverse/pallas_call | solution.py:287
  47.1 9.0 %all-to-all-done.1 = f32[32,32,128]{2,1,0:T(8,128)S(1)} async-done(((f32[32,32,128]{2,1,0:T(8,128)}), f32[32,32,128]{2,1,0:T(8,128)S(1)}, u32[]{:S(2)}, u32[]{:S(2)}) %all-to-all-start.1) | async-done | bytes 524320 | tf_op jit(solution)/shard_map/all_to_all | solution.py:284
  56.1 10.3 %all_to_all.15 = f32[8,32,128]{2,1,0:T(8,128)S(1)} all-to-all(f32[8,32,128]{2,1,0:T(8,128)S(1)} %broadcast_in_dim.2), channel_id=1, replica_groups=mesh['z'=8,'core'=2,'x'=4,'y'=8] {'z'}, dimensions={0} | all-to-all | bytes 262144 | tf_op jit(solution)/shard_map/all_to_all | solution.py:304
  66.4 5.4 %all-gather = f32[64,128]{1,0:T(8,128)S(1)} all-gather(f32[32,128]{1,0:T(8,128)S(1)} %reduce_sum.19), channel_id=2, replica_groups=mesh['z'=8,'core'=2,'x'=4,'y'=8] {'core'}, dimensions={0}, use_global_device_ids=true | all-gather | bytes 49152 | tf_op jit(solution)/shard_map/all_gather | solution.py:307
  71.8 0.0 copy-done
  71.8 1.4 %exposure.1 = (f32[2,64,128]{2,1,0:T(8,128)}, f32[2,64]{1,0:T(2,128)}) custom-call(f32[2,32,128]{2,1,0:T(8,128)S(1)} %bitcast.13, f32[128,128]{1,0:T(8,128)S(1)} %get-tuple-element.18.inverse_ref, bf16[2,64,128]{2,1,0:T(8,128)(2,1)S(1)} %bitcast.12, bf16[128,2048]{1,0:T(8,128)(2,1)S(1)} %get-tuple-element.19.wide_ref), custom_call_target="tpu_custom_call" | custom-call | tf_op jit(solution)/shard_map/exposure/pallas_call | solution.py:308
  (3 shorter events, 0.1 us)
Async XLA Ops:
  1.4 10.9 %copy-start.1 = (bf16[64,4096]{1,0:T(8,128)(2,1)S(1)}, bf16[64,4096]{1,0:T(8,128)(2,1)}, u32[]{:S(2)}) copy-start(bf16[64,4096]{1,0:T(8,128)(2,1)} %coef_ref.1) | copy-start | bytes 1572868
  1.4 10.9 %copy-start.2 = (f32[2,128,16]{1,2,0:T(8,128)S(1)}, f32[2,128,16]{1,2,0:T(8,128)}, u32[]{:S(2)}) copy-start(f32[2,128,16]{1,2,0:T(8,128)} %param.7) | copy-start | bytes 49156
  1.4 10.9 %copy-start.3 = (f32[4096]{0:T(1024)S(1)}, f32[4096]{0:T(1024)}, u32[]{:S(2)}) copy-start(f32[4096]{0:T(1024)} %param.9) | copy-start | bytes 49156
  1.4 10.9 %copy-start.4 = (s32[4096]{0:T(1024)S(1)}, s32[4096]{0:T(1024)}, u32[]{:S(2)}) copy-start(s32[4096]{0:T(1024)} %param.11) | copy-start | bytes 49156
  1.4 10.9 %copy-start.5 = (s32[4096]{0:T(1024)S(1)}, s32[4096]{0:T(1024)}, u32[]{:S(2)}) copy-start(s32[4096]{0:T(1024)} %param.10) | copy-start | bytes 49156
  2.3 28.0 %all-to-all-start = ((f32[8,128,128]{2,1,0:T(8,128)}), f32[8,128,128]{2,1,0:T(8,128)S(1)}, u32[]{:S(2)}, u32[]{:S(2)}) async-start(f32[8,128,128]{2,1,0:T(8,128)} %get-tuple-element.12), calls=%async_computation | async-start | bytes 1048576 | tf_op jit(solution)/shard_map/all_to_all | solution.py:248
  17.0 5.2 %collective-permute-start.1 = (f32[32,32,128]{2,1,0:T(8,128)S(1)}, f32[32,32,128]{2,1,0:T(8,128)S(1)}, u32[]{:S(2)}, u32[]{:S(2)}) collective-permute-start(f32[32,32,128]{2,1,0:T(8,128)S(1)} %get-tuple-element.16), channel_id=1, source_target_pairs={{0,32},{32,0},{1,33},{33,1},{2,34},{34,2},{3,35},{35,3},{4,36},{36... | collective-permute-start | bytes 1572872 | tf_op jit(solution)/shard_map/ppermute | solution.py:264
  30.3 25.8 %all-to-all-start.1 = ((f32[32,32,128]{2,1,0:T(8,128)}), f32[32,32,128]{2,1,0:T(8,128)S(1)}, u32[]{:S(2)}, u32[]{:S(2)}) async-start(f32[32,32,128]{2,1,0:T(8,128)} %pair_moments.1), calls=%async_computation.1 | async-start | bytes 1048576 | tf_op jit(solution)/shard_map/all_to_all | solution.py:284
  39.9 31.9 %copy-start = (bf16[2,128,64]{1,2,0:T(8,128)(2,1)S(1)}, bf16[2,128,64]{1,2,0:T(8,128)(2,1)}, u32[]{:S(2)}) copy-start(bf16[2,128,64]{1,2,0:T(8,128)(2,1)} %param.6) | copy-start | bytes 98308
  39.9 4.5 %collective-permute-start = (f32[8,128,128]{2,1,0:T(8,128)S(1)}, f32[8,128,128]{2,1,0:T(8,128)S(1)}, u32[]{:S(2)}, u32[]{:S(2)}) collective-permute-start(f32[8,128,128]{2,1,0:T(8,128)S(1)} %all-to-all-done.near_ref), channel_id=1, source_target_pairs={{0,32},{32,0},{1,33},{33,1},{2,34},{34,2},{3,35},{35,3},{4,36},{36... | collective-permute-start | bytes 1572872 | tf_op jit(solution)/shard_map/ppermute | solution.py:286
